TPU v7x, 128 devices: a whole 4x4x4 slice. The times are simulated.
128 devices in a mesh: ctx: 16 (over x, z), dp: 8 (over y, core).
Axes of the slice: x: 4, y: 4, z: 4, core: 2. Of those that a mesh axis runs over, the one named last changes fastest.
Arguments:
- queries: bfloat16 [8, 8192, 2048], P('dp', 'ctx'), may hold values from -6 to 6
- keys: bfloat16 [8, 8192, 2048], P('dp', 'ctx'), may hold values from -6 to 6
- values: bfloat16 [8, 8192, 2048], P('dp', 'ctx'), may hold values from -6 to 6
- out_weight: bfloat16 [2048, 2048], replicated, may hold values from -0.125 to 0.125
- out_grad: bfloat16 [8, 8192, 2048], P('dp', 'ctx'), may hold values from -6 to 6
Outputs:
- attended: bfloat16 [8, 8192, 2048], P('dp', 'ctx')
- query_grad: bfloat16 [8, 8192, 2048], P('dp', 'ctx')
- key_grad: bfloat16 [8, 8192, 2048], P('dp', 'ctx')
- value_grad: bfloat16 [8, 8192, 2048], P('dp', 'ctx')
- weight_grad: float32 [2048, 2048], P(('ctx', 'dp'))
All inputs are finite; a program needn't handle non-finite values.
Results may differ from a plain program's by a relative error of at most 0.02.
Values may be sent and summed in bfloat16 or wider, within the bound.
A program may use at most 192 MiB of HBM per device.

v0:
```python
import math

import jax
import jax.numpy as jnp
from jax import lax
from jax.sharding import PartitionSpec as P

DK = 128


def carried_in(array, axis, join, neutral, backward):
    count = lax.axis_size(axis)
    place = lax.axis_index(axis)
    ahead = count - 1 - place if backward else place
    gathered = lax.all_gather(array.astype(jnp.bfloat16), axis)
    state = jnp.zeros_like(array) + jnp.asarray(neutral, array.dtype)

    def one(hop, state):
        source = count - 1 - hop if backward else hop
        return join(state, lax.dynamic_index_in_dim(gathered, source, 0, False).astype(array.dtype))

    return lax.fori_loop(0, ahead, one, state)


def add_states(earlier, later):
    return earlier + later


def on_device(queries, keys, values, out_weight, out_grad):
    tok_rows = queries.shape[1]
    feature_width = queries.shape[2]
    head_count = feature_width // DK
    own_index = lax.axis_index("ctx")
    ctx_count = lax.axis_size("ctx")
    dp_count = lax.axis_size("dp")
    total_tokens = tok_rows * ctx_count * dp_count
    query_heads = queries[0].reshape(tok_rows, head_count, DK)
    key_heads = keys[0].reshape(tok_rows, head_count, DK)
    value_heads = values[0].reshape(tok_rows, head_count, DK)
    positions = own_index * tok_rows + jnp.arange(tok_rows, dtype=jnp.int32)
    factor = lax.rsqrt(((positions + 1) * DK).astype(jnp.float32))[:, None, None]
    row_ids = jnp.arange(tok_rows, dtype=jnp.int32)
    causal = (row_ids[:, None] >= row_ids[None, :])[None]
    empty_state = jnp.zeros((head_count, DK, DK), jnp.float32)
    kv_state = jnp.einsum(
        "thd,the->hde", key_heads, value_heads, preferred_element_type=jnp.float32
    ).astype(jnp.bfloat16)
    grad_out = lax.dot_general(
        out_grad[0], out_weight, (((1,), (1,)), ((), ())), preferred_element_type=jnp.float32
    ).astype(jnp.bfloat16)
    scaled = (grad_out.reshape(tok_rows, head_count, DK).astype(jnp.float32) * factor).astype(
        jnp.bfloat16
    )
    grad_state = jnp.einsum(
        "thd,the->hde", query_heads, scaled, preferred_element_type=jnp.float32
    ).astype(jnp.bfloat16)
    before = carried_in(kv_state.astype(jnp.float32), "ctx", add_states, empty_state, False)
    after = carried_in(grad_state.astype(jnp.float32), "ctx", add_states, empty_state, True)
    before_b = before.astype(jnp.bfloat16)
    after_b = after.astype(jnp.bfloat16)
    scores = jnp.einsum("thd,shd->hts", query_heads, key_heads, preferred_element_type=jnp.float32)
    weights = jnp.where(causal, scores, 0.0).astype(jnp.bfloat16)
    inner = jnp.einsum("hts,she->the", weights, value_heads, preferred_element_type=jnp.float32)
    inner = inner + jnp.einsum(
        "thd,hde->the", query_heads, before_b, preferred_element_type=jnp.float32
    )
    attended = (factor * inner).astype(jnp.bfloat16).reshape(tok_rows, feature_width)
    mixing = jnp.einsum("the,she->hts", scaled, value_heads, preferred_element_type=jnp.float32)
    mixing = jnp.where(causal, mixing, 0.0).astype(jnp.bfloat16)
    query_grad = jnp.einsum("hts,shd->thd", mixing, key_heads, preferred_element_type=jnp.float32)
    query_grad = query_grad + jnp.einsum(
        "the,hde->thd", scaled, before_b, preferred_element_type=jnp.float32
    )
    key_grad = jnp.einsum("hts,thd->shd", mixing, query_heads, preferred_element_type=jnp.float32)
    key_grad = key_grad + jnp.einsum(
        "she,hde->shd", value_heads, after_b, preferred_element_type=jnp.float32
    )
    value_grad = jnp.einsum("hts,the->she", weights, scaled, preferred_element_type=jnp.float32)
    value_grad = value_grad + jnp.einsum(
        "shd,hde->she", key_heads, after_b, preferred_element_type=jnp.float32
    )
    grad_scale = 1.0 / math.sqrt(total_tokens)
    grad_rhs = out_grad[0]
    product = lax.dot_general(
        attended, grad_rhs, (((0,), (0,)), ((), ())), preferred_element_type=jnp.float32
    )
    weight_grad = lax.psum_scatter(
        product * grad_scale, ("ctx", "dp"), scatter_dimension=0, tiled=True
    )
    shape_out = (1, tok_rows, feature_width)
    return (
        attended.reshape(shape_out),
        query_grad.astype(jnp.bfloat16).reshape(shape_out),
        key_grad.astype(jnp.bfloat16).reshape(shape_out),
        value_grad.astype(jnp.bfloat16).reshape(shape_out),
        weight_grad,
    )


def solution(mesh):
    in_specs = (
        P("dp", "ctx", None),
        P("dp", "ctx", None),
        P("dp", "ctx", None),
        P(),
        P("dp", "ctx", None),
    )
    out_specs = (
        P("dp", "ctx", None),
        P("dp", "ctx", None),
        P("dp", "ctx", None),
        P("dp", "ctx", None),
        P(("ctx", "dp"), None),
    )
    return jax.shard_map(
        on_device, mesh=mesh, in_specs=in_specs, out_specs=out_specs, check_vma=False
    )
```

profile of v0, /device:TPU:0, one launch (start us, length us, event | category | flops | bytes accessed | tf_op | source)
XLA Modules:
  0.0 841.5 jit_solution(1860794406269519156)
XLA Ops:
  7.2 3.7 copy.59
  10.9 4.3 copy.35
  15.2 2.4 copy.60
  17.5 1.3 copy-done.6
  18.9 2.0 fusion.24
  20.9 3.5 copy.58
  24.5 9.4 %fusion.4 = f32[512,2048]{1,0:T(8,128)} fusion(bf16[2048,2048]{1,0:T(8,128)(2,1)} %param.12, bf16[1,512,2048]{2,1,0:T(8,128)(2,1)S(1)} %copy-done), kind=kOutput, calls=%fused_computation.15 | convolution fusion | flops 4297064448 | bytes 14680064 | tf_op jit(solution)/shard_map/dot_general | solution.py:48
  33.9 5.6 copy.39
  39.5 3.0 multiply_convert_fusion
  42.5 1.4 copy-done.4
  46.4 5.5 select_convert_fusion.1
  51.9 3.2 copy-done.2
  55.2 4.8 fusion.9
  60.0 34.3 %all-gather.5.cloned.1.call-done = bf16[256,128,128]{2,1,0:T(8,128)(2,1)} async-done(((bf16[16,128,128]{2,1,0:T(8,128)(2,1)}), bf16[256,128,128]{2,1,0:T(8,128)(2,1)}) %all-gather.5.cloned.1.call-update) | async-done | bytes 8388624 | tf_op jit(solution)/shard_map/all_gather | solution.py:15
  94.7 4.2 fusion.3
  98.9 1.3 copy-done.11
  100.3 8.5 %convolution_multiply_fusion = f32[2048,2048]{1,0:T(8,128)} fusion(bf16[512,2048]{0,1:T(8,128)(2,1)S(1)} %bitcast.80, bf16[1,512,2048]{2,1,0:T(8,128)(2,1)S(1)} %copy-done), kind=kOutput, calls=%fused_computation.4 | convolution fusion | flops 4299161600 | bytes 20971520 | tf_op jit(solution)/shard_map/dot_general | solution.py:84
  108.8 1.6 copy-done.5
  110.3 4.5 select_convert_fusion
  114.8 9.6 %fusion.35 = f32[16,128,512]{2,1,0:T(8,128)} fusion(bf16[512,16,128]{0,2,1:T(8,128)(2,1)S(1)} %copy-done.5, bf16[16,512,512]{2,1,0:T(8,128)(2,1)} %copy-done.2), kind=kOutput, calls=%fused_computation.42 | convolution fusion | flops 1073741824 | bytes 14680064 | tf_op jit(solution)/shard_map/hts,the->she/dot_general | solution.py:78
  124.4 4.4 fusion.34
  128.8 2.1 fusion.1
  130.9 3.9 copy.51
  134.8 32.1 %all-gather.7.cloned.1.call-done = bf16[256,128,128]{2,1,0:T(8,128)(2,1)} async-done(((bf16[16,128,128]{2,1,0:T(8,128)(2,1)}), bf16[256,128,128]{2,1,0:T(8,128)(2,1)}) %all-gather.7.cloned.1.call-update) | async-done | bytes 8388624 | tf_op jit(solution)/shard_map/all_gather | solution.py:15
  167.1 19.9 %while.23 = (s32[]{:T(128)}, f32[16,128,128]{2,1,0:T(8,128)S(1)}, s32[]{:T(128)}, bf16[16,16,128,128]{3,2,1,0:T(8,128)(2,1)}, s32[]{:T(128)}, /*index=5*/s32[]{:T(128)}, s32[]{:T(128)}, s32[]{:T(128)}) while((s32[]{:T(128)}, f32[16,128,128]{2,1,0:T(8,128)S(1)}, s32[]{:T(128)}, bf16[16,16,128,128]{3,2,1,0:T(8,128)(2,1)}, s32[]{:T(128)}, ...), condition=%wide.region_3.4_spmd, body=%wide.region_2.3_spmd.sunk | while | flops 524294 | bytes 2621583 | solution.py:22
  186.9 2.7 fusion.11
  189.7 6.6 fusion
  196.3 3.9 copy.52
  200.2 5.5 add_convert_fusion
  205.7 3.9 copy.53
  209.6 4.1 copy.50
  213.7 621.3 %reduce-scatter.2.cloned.1.call-done = f32[16,2048]{1,0:T(8,128)} async-done(((f32[2048,2048]{1,0:T(8,128)}), f32[16,2048]{1,0:T(8,128)}) %reduce-scatter.2.cloned.1.call-update) | async-done | bytes 131088 | tf_op jit(solution)/shard_map/reduce_scatter | solution.py:87
  (47 shorter events, 22.4 us)
Async XLA Ops:
  7.2 17.3 %copy-start = (bf16[1,512,2048]{2,1,0:T(8,128)(2,1)S(1)}, bf16[1,512,2048]{2,1,0:T(8,128)(2,1)}, u32[]{:S(2)}) copy-start(bf16[1,512,2048]{2,1,0:T(8,128)(2,1)} %param.13) | copy-start | bytes 6291460
  7.2 87.2 %all-gather.5.cloned.1.call-start = ((), (), s32[]{:S(2)}) async-start(), calls=%async_computation.2 | async-start | bytes 8912896 | tf_op jit(solution)/shard_map/all_gather | solution.py:15
  15.2 3.7 copy-start.10
  17.5 1.3 copy-start.6
  20.9 146.1 %all-gather.7.cloned.1.call-start = ((), (), s32[]{:S(2)}) async-start(), calls=%async_computation.3 | async-start | bytes 8912896 | tf_op jit(solution)/shard_map/all_gather | solution.py:15
  39.5 4.4 copy-start.8
  42.5 1.4 copy-start.4
  46.1 788.9 %reduce-scatter.2.cloned.1.call-start = ((), (), s32[]{:S(2)}) async-start(), calls=%async_computation.1 | async-start | bytes 16908288 | tf_op jit(solution)/shard_map/reduce_scatter | solution.py:87
  46.4 8.7 %copy-start.7 = (bf16[64,8,16,128]{3,2,1,0:T(8,128)(2,1)S(1)}, bf16[64,8,16,128]{3,2,1,0:T(8,128)(2,1)}, u32[]{:S(2)}) copy-start(bf16[64,8,16,128]{3,2,1,0:T(8,128)(2,1)} %copy-done.6) | copy-start | bytes 6291460
  51.9 3.2 copy-start.2
  98.9 1.3 copy-start.11
  108.7 1.6 copy-start.5
  114.8 9.7 %copy-start.3 = (bf16[16,512,512]{2,1,0:T(8,128)(2,1)}, bf16[16,512,512]{2,1,0:T(8,128)(2,1)S(1)}, u32[]{:S(2)}) copy-start(bf16[16,512,512]{2,1,0:T(8,128)(2,1)S(1)} %select_convert_fusion) | copy-start | bytes 25165828
  186.9 2.8 copy-start.9
  209.6 625.4 %copy-start.1 = (bf16[1,512,2048]{2,1,0:T(8,128)(2,1)S(1)}, bf16[1,512,2048]{2,1,0:T(8,128)(2,1)}, u32[]{:S(2)}) copy-start(bf16[1,512,2048]{2,1,0:T(8,128)(2,1)} %param.13) | copy-start | bytes 6291460
Sparse Core Ops, SparseCore 0:
  21.0 73.3 all-gather.4
  96.5 70.4 all-gather.6
  169.9 665.0 reduce-scatter.1
where the time goes:
time: 843 us; the launch traced here: 841 us
  waiting for transfers between devices  688 us (82%)
  matrix products  71 us (8%)
  local copies, waits for them, and re-layouts  45.3 us (5%)
  other arithmetic  22.4 us (3%)
  between operations  13.9 us (2%)
    reduce_scatter x1, waiting for transfers between devices, on_device(): lax.psum_scatter(product * grad_scale, ('ctx', 'dp'), scatter_dimension=0...  621 us
    all_gather x2, waiting for transfers between devices, carried_in(): gathered = lax.all_gather(array.astype(jnp.bfloat16), axis)  66.5 us
    unnamed x31, local copies, waits for them, and re-layouts  34.2 us
    add x15, other arithmetic, add_states(): return earlier + later  19.3 us
  transfers between devices with their start and end apart: 3, of which 3 were waited for; matrix products, arithmetic and copies ran while one was open for 14% of the time, Pallas kernels for 0%

commit v1 on v0

v1 whole, which is shorter than its diff:
```python
import functools
import math

import jax
import jax.numpy as jnp
from jax import lax
from jax.experimental import pallas as pl
from jax.experimental.pallas import tpu as pltpu
from jax.sharding import PartitionSpec as P

DK = 128
CH = 256
MESH = pl.DeviceIdType.MESH
BF = jnp.bfloat16
F32 = jnp.float32
PIECES = (
    (0, 384, "yxz"),
    (384, 384, "xzy"),
    (768, 384, "zyx"),
    (1152, 384, "yzx"),
    (1536, 256, "xyz"),
    (1792, 256, "zxy"),
)
AXES = "xzy"


def dot_nn(a, b):
    return lax.dot_general(a, b, (((1,), (0,)), ((), ())), preferred_element_type=F32)


def dot_nt(a, b):
    return lax.dot_general(a, b, (((1,), (1,)), ((), ())), preferred_element_type=F32)


def dot_tn(a, b):
    return lax.dot_general(a, b, (((0,), (0,)), ((), ())), preferred_element_type=F32)


def head_cols(h):
    return pl.ds(pl.multiple_of(h * DK, DK), DK)


def causal_mask():
    rows = lax.broadcasted_iota(jnp.int32, (CH, CH), 0)
    cols = lax.broadcasted_iota(jnp.int32, (CH, CH), 1)
    return rows >= cols


def token_factor(me, first, rows):
    pos = me * 512 + first + lax.broadcasted_iota(jnp.int32, (rows, DK), 0)
    return lax.rsqrt(((pos + 1) * DK).astype(F32))


def main_kernel(
    grad_scale,
    q_hbm, k_hbm, v_hbm, w_hbm, og_hbm,
    att_hbm, scaled_hbm, before_hbm, after_hbm, wgrad_hbm,
    qb, kb, vb, wb, ogb, og_mate, scaled, inner, att, att_t, mate_t,
    s1, tx_kv, rx_kv, px_kv, before, tx_g, rx_g, px_g, after, wgrad,
    prod, rx1, sum1, rx2, sum2, rx3,
    in_sem, out_sem, og_sem, kv1_s, kv1_r, kv2_s, kv2_r, g1_s, g1_r, g2_s, g2_r,
    mate_s, mate_r, rs_s, rs_r,
):
    me = lax.axis_index("ctx")
    dp = lax.axis_index("dp")
    place = {"x": me // 4, "z": me % 4, "y": dp // 2}
    core = dp % 2
    mate = (me, (dp // 2) * 2 + (1 - core))
    count = 16

    def axis_peer(axis, offset):
        at = dict(place)
        at[axis] = (place[axis] + offset) % 4
        return (at["x"] * 4 + at["z"], at["y"] * 2 + core)

    loads = [
        pltpu.make_async_copy(src.at[0], dst, in_sem.at[n])
        for n, (src, dst) in enumerate(((k_hbm, kb), (v_hbm, vb), (og_hbm, ogb), (q_hbm, qb)))
    ]
    loads.append(pltpu.make_async_copy(w_hbm, wb, in_sem.at[4]))
    loads[0].start()
    loads[1].start()
    loads[2].start()
    loads[4].start()
    loads[3].start()

    barrier = pltpu.get_barrier_semaphore()
    for offset in range(1, count):
        pl.semaphore_signal(
            barrier, inc=1, device_id=((me + offset) % count, dp), device_id_type=MESH
        )
    pl.semaphore_signal(barrier, inc=1, device_id=mate, device_id_type=MESH)
    for offset in range(1, 4):
        pl.semaphore_signal(
            barrier, inc=1, device_id=axis_peer("y", offset), device_id_type=MESH
        )

    loads[0].wait()
    loads[1].wait()

    def kv_one(h, carry):
        cols = head_cols(h)
        first = dot_tn(kb[0:CH, cols], vb[0:CH, cols])
        second = dot_tn(kb[CH : 2 * CH, cols], vb[CH : 2 * CH, cols])
        s1[h] = first.astype(BF)
        tx_kv[h] = (first + second).astype(BF)
        return carry

    lax.fori_loop(0, count, kv_one, 0)
    rx_kv[me] = tx_kv[me]
    pl.semaphore_wait(barrier, count - 1 + 1 + 3)

    def exchange(src, dst, send, recv, offset):
        other = (me + offset) % count
        return pltpu.make_async_remote_copy(
            src_ref=src.at[other], dst_ref=dst.at[me], send_sem=send.at[other],
            recv_sem=recv.at[me], device_id=(other, dp), device_id_type=MESH,
        )

    def arrival(src, dst, send, recv, other):
        return pltpu.make_async_remote_copy(
            src_ref=src.at[other], dst_ref=dst.at[other], send_sem=send.at[other],
            recv_sem=recv.at[other], device_id=(other, dp), device_id_type=MESH,
        )

    def send_all(src, dst, send, recv):
        def one(offset, carry):
            exchange(src, dst, send, recv, offset).start()
            return carry

        lax.fori_loop(1, count, one, 0)

    send_all(tx_kv, rx_kv, kv1_s, kv1_r)

    loads[2].wait()
    og_copy = pltpu.make_async_remote_copy(
        src_ref=ogb, dst_ref=og_mate, send_sem=og_sem.at[0], recv_sem=og_sem.at[1],
        device_id=mate, device_id_type=MESH,
    )
    og_copy.start()

    loads[4].wait()
    loads[3].wait()

    def grad_one(j, carry):
        wide = pl.ds(pl.multiple_of(j * 256, 256), 256)
        grad_out = dot_nt(ogb[...], wb[wide, :]).astype(BF).astype(F32)
        factor = token_factor(me, 0, 512)
        for n in range(2):
            cols = head_cols(2 * j + n)
            here = (grad_out[:, n * DK : (n + 1) * DK] * factor).astype(BF)
            scaled[:, cols] = here
            tx_g[2 * j + n] = dot_tn(qb[:, cols], here).astype(BF)
        return carry

    lax.fori_loop(0, count // 2, grad_one, 0)
    scaled_out = pltpu.make_async_copy(scaled, scaled_hbm, out_sem.at[0])
    scaled_out.start()
    rx_g[me] = tx_g[me]
    send_all(tx_g, rx_g, g1_s, g1_r)

    def scan(src, dst, send, recv, src2, dst2, send2, recv2, reverse):
        def one(n, total):
            b = count - 1 - n if reverse else n

            @pl.when(b != me)
            def _():
                arrival(src, dst, send, recv, b).wait_recv()

            src2[b] = total.astype(BF)

            @pl.when(b != me)
            def _():
                pltpu.make_async_remote_copy(
                    src_ref=src2.at[b], dst_ref=dst2.at[me], send_sem=send2.at[b],
                    recv_sem=recv2.at[me], device_id=(b, dp), device_id_type=MESH,
                ).start()

            return total + dst[b].astype(F32)

        lax.fori_loop(0, count, one, jnp.zeros((DK, DK), F32))
        dst2[me] = src2[me]

    def finish(src, dst, send, recv, which):
        def one(offset, carry):
            other = (me + offset) % count
            if which == "recv":
                arrival(src, dst, send, recv, other).wait_recv()
            else:
                arrival(src, dst, send, recv, other).wait_send()
            return carry

        lax.fori_loop(1, count, one, 0)

    scan(tx_kv, rx_kv, kv1_s, kv1_r, px_kv, before, kv2_s, kv2_r, False)

    def inner_one(h, carry):
        cols = head_cols(h)
        mask = causal_mask()
        for c in range(2):
            rows = pl.ds(c * CH, CH)
            weights = jnp.where(mask, dot_nt(qb[rows, cols], kb[rows, cols]), 0.0).astype(BF)
            part = dot_nn(weights, vb[rows, cols])
            if c == 1:
                part = part + dot_nn(qb[rows, cols], s1[h])
            inner[rows, cols] = part
        return carry

    lax.fori_loop(0, count, inner_one, 0)

    scan(tx_g, rx_g, g1_s, g1_r, px_g, after, g2_s, g2_r, True)

    finish(px_kv, before, kv2_s, kv2_r, "recv")
    before_out = pltpu.make_async_copy(before, before_hbm, out_sem.at[1])
    before_out.start()

    def mate_copy(h):
        return pltpu.make_async_remote_copy(
            src_ref=att_t.at[1 - core, h], dst_ref=mate_t.at[h], send_sem=mate_s.at[h],
            recv_sem=mate_r.at[h], device_id=mate, device_id_type=MESH,
        )

    def att_one(h, carry):
        cols = head_cols(h)
        for c in range(2):
            rows = pl.ds(c * CH, CH)
            total = inner[rows, cols] + dot_nn(qb[rows, cols], before[h])
            total = total * token_factor(me, c * CH, CH)
            att[rows, cols] = total.astype(BF)
            turned = total.T.astype(BF)
            for y in range(4):
                for n in range(2):
                    first = y * 32 + n * 16
                    att_t[n, h, y, :, c * CH : (c + 1) * CH] = turned[first : first + 16]
        mate_copy(h).start()
        return carry

    lax.fori_loop(0, count, att_one, 0)
    att_out = pltpu.make_async_copy(att, att_hbm, out_sem.at[2])
    att_out.start()

    og_copy.wait()

    def mate_wait(h, carry):
        mate_copy(h).wait()
        return carry

    lax.fori_loop(0, count, mate_wait, 0)

    def pick(ref, axes, axis, t):
        index = tuple(t if a == axis else slice(None) for a in axes)
        return ref.at[index]

    def rs_copy(p, phase, offset):
        first, width, order = PIECES[p]
        axes = [a for a in AXES if a not in order[:phase]]
        axis = order[phase]
        src = (prod, sum1, sum2)[phase][p]
        dst = (rx1, rx2, rx3)[phase][p]
        return pltpu.make_async_remote_copy(
            src_ref=pick(src, axes, axis, (place[axis] + offset) % 4),
            dst_ref=dst.at[offset - 1],
            send_sem=rs_s.at[phase, p, offset - 1],
            recv_sem=rs_r.at[phase, p, offset - 1],
            device_id=axis_peer(axis, offset), device_id_type=MESH,
        )

    def rs_sum(p, phase):
        first, width, order = PIECES[p]
        axes = [a for a in AXES if a not in order[:phase]]
        axis = order[phase]
        for offset in range(1, 4):
            rs_copy(p, phase, offset).wait_recv()
        src = (prod, sum1, sum2)[phase][p]
        dst = (rx1, rx2, rx3)[phase][p]
        total = pick(src, axes, axis, place[axis])[...].astype(F32)
        for n in range(3):
            total = total + dst[n].astype(F32)
        return total

    for p, (first, width, order) in enumerate(PIECES):
        def prod_half(n, carry, p=p, first=first, width=width):
            rows = pl.ds(n * 8, 8)
            left = att_t[core, rows].reshape(512, 512)
            part = dot_nn(left, ogb[:, first : first + width])
            other = mate_t[rows].reshape(512, 512)
            part = part + dot_nn(other, og_mate[:, first : first + width])
            prod[p][pl.ds(n * 2, 2)] = part.astype(BF).reshape(2, 4, 4, 16, width)
            return carry

        lax.fori_loop(0, 2, prod_half, 0)
        for offset in range(1, 4):
            rs_copy(p, 0, offset).start()

    finish(px_g, after, g2_s, g2_r, "recv")
    after_out = pltpu.make_async_copy(after, after_hbm, out_sem.at[3])
    after_out.start()

    for p in range(len(PIECES)):
        sum1[p][...] = rs_sum(p, 0).astype(BF)
        for offset in range(1, 4):
            rs_copy(p, 1, offset).start()
    for p in range(len(PIECES)):
        sum2[p][...] = rs_sum(p, 1).astype(BF)
        for offset in range(1, 4):
            rs_copy(p, 2, offset).start()
    for p, (first, width, order) in enumerate(PIECES):
        wgrad[:, first : first + width] = rs_sum(p, 2) * grad_scale
    wgrad_out = pltpu.make_async_copy(wgrad, wgrad_hbm, out_sem.at[4])
    wgrad_out.start()

    finish(tx_kv, rx_kv, kv1_s, kv1_r, "send")
    finish(tx_g, rx_g, g1_s, g1_r, "send")
    finish(px_kv, before, kv2_s, kv2_r, "send")
    finish(px_g, after, g2_s, g2_r, "send")
    for p in range(len(PIECES)):
        for phase in range(3):
            for offset in range(1, 4):
                rs_copy(p, phase, offset).wait_send()
    scaled_out.wait()
    before_out.wait()
    att_out.wait()
    after_out.wait()
    wgrad_out.wait()


def main_call(q, k, v, w, og, grad_scale):
    any_spec = pl.BlockSpec(memory_space=pl.ANY)
    n = len(PIECES)
    widths = [width for _, width, _ in PIECES]
    vm = pltpu.VMEM
    sem = pltpu.SemaphoreType.DMA
    state = vm((16, DK, DK), BF)
    scratch = [
        vm((512, 2048), BF), vm((512, 2048), BF), vm((512, 2048), BF), vm((2048, 2048), BF),
        vm((512, 2048), BF), vm((512, 2048), BF), vm((512, 2048), BF), vm((512, 2048), F32),
        vm((512, 2048), BF), vm((2, 16, 4, 16, 512), BF), vm((16, 4, 16, 512), BF),
        state, state, state, state, state, state, state, state, state, vm((16, 2048), F32),
        [vm((4, 4, 4, 16, c), BF) for c in widths],
        [vm((3, 4, 4, 16, c), BF) for c in widths],
        [vm((4, 4, 16, c), BF) for c in widths],
        [vm((3, 4, 16, c), BF) for c in widths],
        [vm((4, 16, c), BF) for c in widths],
        [vm((3, 16, c), BF) for c in widths],
        sem((5,)), sem((5,)), sem((2,)),
        sem((16,)), sem((16,)), sem((16,)), sem((16,)),
        sem((16,)), sem((16,)), sem((16,)), sem((16,)),
        sem((16,)), sem((16,)), sem((3, n, 3)), sem((3, n, 3)),
    ]
    return pl.pallas_call(
        functools.partial(main_kernel, grad_scale),
        out_shape=(
            jax.ShapeDtypeStruct((512, 2048), BF),
            jax.ShapeDtypeStruct((512, 2048), BF),
            jax.ShapeDtypeStruct((16, DK, DK), BF),
            jax.ShapeDtypeStruct((16, DK, DK), BF),
            jax.ShapeDtypeStruct((16, 2048), F32),
        ),
        in_specs=[any_spec] * 5,
        out_specs=(any_spec,) * 5,
        scratch_shapes=scratch,
        compiler_params=pltpu.CompilerParams(
            collective_id=1, has_side_effects=True, vmem_limit_bytes=56 << 20
        ),
        name="states_and_weight_grad",
    )(q, k, v, w, og)


def grads_kernel(q, k, v, s, before, after, att_hbm, qg, kg, vg, att_out, sem):
    step = pl.program_id(0)
    copy = pltpu.make_async_copy(att_hbm, att_out.at[0], sem)

    @pl.when(step == 0)
    def _():
        copy.start()

    mask = causal_mask()
    low, high = slice(0, CH), slice(CH, 2 * CH)
    for n in range(2):
        cols = slice(n * DK, (n + 1) * DK)
        early = dot_tn(k[0, low, cols], v[0, low, cols])
        late = dot_tn(q[0, high, cols], s[high, cols])
        before_of = (before[n], (before[n].astype(F32) + early).astype(BF))
        after_of = ((after[n].astype(F32) + late).astype(BF), after[n])
        for c, rows in enumerate((low, high)):
            qc, kc, vc, sc = q[0, rows, cols], k[0, rows, cols], v[0, rows, cols], s[rows, cols]
            weights = jnp.where(mask, dot_nt(qc, kc), 0.0).astype(BF)
            mixing = jnp.where(mask, dot_nt(sc, vc), 0.0).astype(BF)
            qg[0, rows, cols] = (dot_nn(mixing, kc) + dot_nt(sc, before_of[c])).astype(BF)
            kg[0, rows, cols] = (dot_tn(mixing, qc) + dot_nt(vc, after_of[c])).astype(BF)
            vg[0, rows, cols] = (dot_tn(weights, sc) + dot_nn(kc, after_of[c])).astype(BF)

    @pl.when(step == pl.num_programs(0) - 1)
    def _():
        copy.wait()


def grads_call(q, k, v, s, before, after, att):
    big = pl.BlockSpec((1, 512, 256), lambda j: (0, 0, j))
    flat = pl.BlockSpec((512, 256), lambda j: (0, j))
    state = pl.BlockSpec((2, DK, DK), lambda j: (j, 0, 0))
    any_spec = pl.BlockSpec(memory_space=pl.ANY)
    shape = jax.ShapeDtypeStruct((1, 512, 2048), BF)
    return pl.pallas_call(
        grads_kernel,
        grid=(8,),
        out_shape=(shape,) * 4,
        in_specs=[big, big, big, flat, state, state, any_spec],
        out_specs=(big, big, big, any_spec),
        scratch_shapes=[pltpu.SemaphoreType.DMA],
        compiler_params=pltpu.CompilerParams(vmem_limit_bytes=32 << 20),
        name="input_grads",
    )(q, k, v, s, before, after, att)


def on_device(queries, keys, values, out_weight, out_grad):
    grad_scale = 1.0 / math.sqrt(8 * 8192)
    att, scaled, before, after, weight_grad = main_call(
        queries, keys, values, out_weight, out_grad, grad_scale
    )
    query_grad, key_grad, value_grad, attended = grads_call(
        queries, keys, values, scaled, before, after, att
    )
    return attended, query_grad, key_grad, value_grad, weight_grad


def solution(mesh):
    tokens = P("dp", "ctx", None)
    return jax.shard_map(
        on_device,
        mesh=mesh,
        in_specs=(tokens, tokens, tokens, P(), tokens),
        out_specs=(tokens, tokens, tokens, tokens, P(("ctx", "dp"), None)),
        check_vma=False,
    )
```

time: 843 us -> 101 us (0.12)
  waiting for transfers between devices: 688 us -> 0 us
  Pallas kernels: 0 us -> 94.3 us
  matrix products: 71 us -> 0 us
  local copies, waits for them, and re-layouts: 45.3 us -> 5.93 us
  other arithmetic: 22.4 us -> 0 us
  between operations: 13.9 us -> 0.72 us
    reduce_scatter x1 -> x0, waiting for transfers between devices: 621 us -> none  [on_device(): lax.psum_scatter(product * grad_scale, ('ctx', 'dp'), scatter_dimension=0...]
    pallas_call x0 -> x2, Pallas kernels: none -> 94.3 us  [the longest x1 79.6 us: main_call(): pl.pallas_call(functools.partial(main_kernel, grad_scale), out_shape=(jax...]
    dot_general x14 -> x0, matrix products: 71 us -> none  [the longest x1 9.64 us: on_device(): jnp.einsum('hts,the->she', weights, scaled, preferred_element_type=jnp.fl...]
    all_gather x2 -> x0, waiting for transfers between devices: 66.5 us -> none  [carried_in(): gathered = lax.all_gather(array.astype(jnp.bfloat16), axis)]
    unnamed x31 -> x17, local copies, waits for them, and re-layouts: 34.2 us -> 5.93 us
    add x15 -> x0, other arithmetic: 19.3 us -> none  [add_states(): return earlier + later]
  transfers between devices with their start and end apart: 3 -> 0, of which waited for: 3 -> 0; matrix products, arithmetic and copies ran while one was open for 14% -> 0% of each run, Pallas kernels for 0% -> 0%
where the time goes in v1:
time: 101 us
  Pallas kernels  94.3 us (93%)
  local copies, waits for them, and re-layouts  5.93 us (6%)
    pallas_call x1, Pallas kernels, main_call(): pl.pallas_call(functools.partial(main_kernel, grad_scale), out_shape=(jax...  79.6 us
    pallas_call x1, Pallas kernels, grads_call(): pl.pallas_call(grads_kernel, grid=(8,), out_shape=(shape,) * 4, in_specs=...  14.6 us
    unnamed x17, local copies, waits for them, and re-layouts  5.93 us

profile of v1, /device:TPU:0, one launch (start us, length us, event | category | flops | bytes accessed | tf_op | source)
XLA Modules:
  0.0 100.9 jit_solution(4885595953959915433)
XLA Ops:
  0.6 0.0 copy-start.2
  0.6 0.0 copy-start.1
  0.7 0.0 copy-start
  0.7 79.6 %states_and_weight_grad.1 = (bf16[512,2048]{1,0:T(8,128)(2,1)}, bf16[512,2048]{1,0:T(8,128)(2,1)}, bf16[16,128,128]{2,1,0:T(8,128)(2,1)}, bf16[16,128,128]{2,1,0:T(8,128)(2,1)}, f32[16,2048]{1,0:T(8,128)}) custom-call(bf16[1,512,2048]{2,1,0:T(8,128)(2,1)} %q.1, bf16[1,512,2048]{2,1,0:T(8,128)(2,1)} %k.1, bf16[1,512,2048]{2,1,0:T(8,128)(2,1)} %v.1, ...), custom_call_target="tpu_custom_call" | custom-call | tf_op jit(solution)/shard_map/states_and_weight_grad/pallas_call | solution.py:350
  80.3 0.0 copy-done.2
  80.3 0.0 copy-done.1
  80.3 0.0 copy-done
  80.3 0.0 copy-start.3
  80.4 1.6 %copy-done.3 = bf16[512,2048]{1,0:T(8,128)(2,1)S(1)} copy-done((bf16[512,2048]{1,0:T(8,128)(2,1)S(1)}, bf16[512,2048]{1,0:T(8,128)(2,1)}, u32[]{:S(2)}) %copy-start.3) | copy-done | bytes 2097176
  81.9 0.0 copy-start.4
  81.9 1.6 %copy-done.4 = bf16[512,2048]{1,0:T(8,128)(2,1)S(1)} copy-done((bf16[512,2048]{1,0:T(8,128)(2,1)S(1)}, bf16[512,2048]{1,0:T(8,128)(2,1)}, u32[]{:S(2)}) %copy-start.4) | copy-done | bytes 2097176
  83.5 0.0 copy-start.5
  83.5 1.0 %copy-done.5 = bf16[16,128,128]{2,1,0:T(8,128)(2,1)S(1)} copy-done((bf16[16,128,128]{2,1,0:T(8,128)(2,1)S(1)}, bf16[16,128,128]{2,1,0:T(8,128)(2,1)}, u32[]{:S(2)}) %copy-start.5) | copy-done | bytes 524312
  84.6 0.0 copy-start.6
  84.6 1.0 %copy-done.6 = bf16[16,128,128]{2,1,0:T(8,128)(2,1)S(1)} copy-done((bf16[16,128,128]{2,1,0:T(8,128)(2,1)S(1)}, bf16[16,128,128]{2,1,0:T(8,128)(2,1)}, u32[]{:S(2)}) %copy-start.6) | copy-done | bytes 524312
  85.6 0.0 copy-start.7
  85.6 14.6 %input_grads.1 = (bf16[1,512,2048]{2,1,0:T(8,128)(2,1)}, bf16[1,512,2048]{2,1,0:T(8,128)(2,1)}, bf16[1,512,2048]{2,1,0:T(8,128)(2,1)}, bf16[1,512,2048]{2,1,0:T(8,128)(2,1)}) custom-call(bf16[1,512,2048]{2,1,0:T(8,128)(2,1)S(1)} %copy-done, bf16[1,512,2048]{2,1,0:T(8,128)(2,1)S(1)} %copy-done.1, bf16[1,512,2048]{2,1,0:T(8,128)(2,1)S(1)} %copy-done.2, ...), custom_call_target="tpu_custom_call" | custom-call | tf_op jit(solution)/shard_map/input_grads/pallas_call | solution.py:404
  100.3 0.0 copy-done.7
  100.3 0.7 copy.11
Async XLA Ops:
  0.6 79.7 %copy-start.2 = (bf16[1,512,2048]{2,1,0:T(8,128)(2,1)S(1)}, bf16[1,512,2048]{2,1,0:T(8,128)(2,1)}, u32[]{:S(2)}) copy-start(bf16[1,512,2048]{2,1,0:T(8,128)(2,1)} %v.1) | copy-start | bytes 6291460
  0.6 79.7 %copy-start.1 = (bf16[1,512,2048]{2,1,0:T(8,128)(2,1)S(1)}, bf16[1,512,2048]{2,1,0:T(8,128)(2,1)}, u32[]{:S(2)}) copy-start(bf16[1,512,2048]{2,1,0:T(8,128)(2,1)} %k.1) | copy-start | bytes 6291460
  0.7 79.7 %copy-start = (bf16[1,512,2048]{2,1,0:T(8,128)(2,1)S(1)}, bf16[1,512,2048]{2,1,0:T(8,128)(2,1)}, u32[]{:S(2)}) copy-start(bf16[1,512,2048]{2,1,0:T(8,128)(2,1)} %q.1) | copy-start | bytes 6291460
  80.3 1.6 %copy-start.3 = (bf16[512,2048]{1,0:T(8,128)(2,1)S(1)}, bf16[512,2048]{1,0:T(8,128)(2,1)}, u32[]{:S(2)}) copy-start(bf16[512,2048]{1,0:T(8,128)(2,1)} %get-tuple-element.17.att_hbm) | copy-start | bytes 6291460
  81.9 1.6 %copy-start.4 = (bf16[512,2048]{1,0:T(8,128)(2,1)S(1)}, bf16[512,2048]{1,0:T(8,128)(2,1)}, u32[]{:S(2)}) copy-start(bf16[512,2048]{1,0:T(8,128)(2,1)} %get-tuple-element.14.s) | copy-start | bytes 6291460
  83.5 1.0 %copy-start.5 = (bf16[16,128,128]{2,1,0:T(8,128)(2,1)S(1)}, bf16[16,128,128]{2,1,0:T(8,128)(2,1)}, u32[]{:S(2)}) copy-start(bf16[16,128,128]{2,1,0:T(8,128)(2,1)} %get-tuple-element.15.before) | copy-start | bytes 1572868
  84.6 1.0 %copy-start.6 = (bf16[16,128,128]{2,1,0:T(8,128)(2,1)S(1)}, bf16[16,128,128]{2,1,0:T(8,128)(2,1)}, u32[]{:S(2)}) copy-start(bf16[16,128,128]{2,1,0:T(8,128)(2,1)} %get-tuple-element.16.after) | copy-start | bytes 1572868
  85.6 14.7 %copy-start.7 = (f32[16,2048]{1,0:T(8,128)S(1)}, f32[16,2048]{1,0:T(8,128)}, u32[]{:S(2)}) copy-start(f32[16,2048]{1,0:T(8,128)} %get-tuple-element.32) | copy-start | bytes 393220

commit v2 on v1

--- a/solution.py
+++ b/solution.py
@@ -14,12 +14,15 @@
 BF = jnp.bfloat16
 F32 = jnp.float32
 PIECES = (
-    (0, 384, "yxz"),
-    (384, 384, "xzy"),
-    (768, 384, "zyx"),
-    (1152, 384, "yzx"),
-    (1536, 256, "xyz"),
-    (1792, 256, "zxy"),
+    (0, 256, "yxz"),
+    (256, 256, "xzy"),
+    (512, 256, "zyx"),
+    (768, 256, "yzx"),
+    (1024, 256, "xyz"),
+    (1280, 256, "zxy"),
+    (1536, 256, "yxz"),
+    (1792, 128, "xzy"),
+    (1920, 128, "zyx"),
 )
 AXES = "xzy"
 
@@ -40,23 +43,24 @@
     return pl.ds(pl.multiple_of(h * DK, DK), DK)
 
 
-def causal_mask():
+def masked(product, query_rows):
     rows = lax.broadcasted_iota(jnp.int32, (CH, CH), 0)
     cols = lax.broadcasted_iota(jnp.int32, (CH, CH), 1)
-    return rows >= cols
-
-
-def token_factor(me, first, rows):
-    pos = me * 512 + first + lax.broadcasted_iota(jnp.int32, (rows, DK), 0)
+    keep = rows >= cols if query_rows else rows <= cols
+    return jnp.where(keep, product, 0.0).astype(BF)
+
+
+def token_factor(me, shape, axis):
+    pos = me * 512 + lax.broadcasted_iota(jnp.int32, shape, axis)
     return lax.rsqrt(((pos + 1) * DK).astype(F32))
 
 
 def main_kernel(
     grad_scale,
     q_hbm, k_hbm, v_hbm, w_hbm, og_hbm,
-    att_hbm, scaled_hbm, before_hbm, after_hbm, wgrad_hbm,
-    qb, kb, vb, wb, ogb, og_mate, scaled, inner, att, att_t, mate_t,
-    s1, tx_kv, rx_kv, px_kv, before, tx_g, rx_g, px_g, after, wgrad,
+    att_hbm, qg_hbm, kg_hbm, vg_hbm, wgrad_hbm,
+    qb, kb, vb, wb, ogb, og_mate, scaled, inner_t, att, att_full, att_t, mate_t, weights_t,
+    s1, g2, tx_kv, rx_kv, px_kv, before, tx_g, rx_g, px_g, after, wgrad,
     prod, rx1, sum1, rx2, sum2, rx3,
     in_sem, out_sem, og_sem, kv1_s, kv1_r, kv2_s, kv2_r, g1_s, g1_r, g2_s, g2_r,
     mate_s, mate_r, rs_s, rs_r,
@@ -98,15 +102,19 @@
     loads[0].wait()
     loads[1].wait()
 
-    def kv_one(h, carry):
-        cols = head_cols(h)
-        first = dot_tn(kb[0:CH, cols], vb[0:CH, cols])
-        second = dot_tn(kb[CH : 2 * CH, cols], vb[CH : 2 * CH, cols])
-        s1[h] = first.astype(BF)
-        tx_kv[h] = (first + second).astype(BF)
-        return carry
-
-    lax.fori_loop(0, count, kv_one, 0)
+    low, high = slice(0, CH), slice(CH, 2 * CH)
+
+    def kv_one(j, carry):
+        wide = pl.ds(pl.multiple_of(j * 256, 256), 256)
+        first = dot_tn(vb[low, wide], kb[low, wide])
+        both = first + dot_tn(vb[high, wide], kb[high, wide])
+        for n in range(2):
+            part = slice(n * DK, (n + 1) * DK)
+            s1[2 * j + n] = first[part, part].astype(BF)
+            tx_kv[2 * j + n] = both[part, part].astype(BF)
+        return carry
+
+    lax.fori_loop(0, count // 2, kv_one, 0)
     rx_kv[me] = tx_kv[me]
     pl.semaphore_wait(barrier, count - 1 + 1 + 3)
 
@@ -145,17 +153,16 @@
     def grad_one(j, carry):
         wide = pl.ds(pl.multiple_of(j * 256, 256), 256)
         grad_out = dot_nt(ogb[...], wb[wide, :]).astype(BF).astype(F32)
-        factor = token_factor(me, 0, 512)
+        scaled[:, wide] = (grad_out * token_factor(me, (512, 256), 0)).astype(BF)
+        late = dot_tn(qb[high, wide], scaled[high, wide])
+        both = late + dot_tn(qb[low, wide], scaled[low, wide])
         for n in range(2):
-            cols = head_cols(2 * j + n)
-            here = (grad_out[:, n * DK : (n + 1) * DK] * factor).astype(BF)
-            scaled[:, cols] = here
-            tx_g[2 * j + n] = dot_tn(qb[:, cols], here).astype(BF)
+            part = slice(n * DK, (n + 1) * DK)
+            g2[2 * j + n] = late[part, part].astype(BF)
+            tx_g[2 * j + n] = both[part, part].astype(BF)
         return carry
 
     lax.fori_loop(0, count // 2, grad_one, 0)
-    scaled_out = pltpu.make_async_copy(scaled, scaled_hbm, out_sem.at[0])
-    scaled_out.start()
     rx_g[me] = tx_g[me]
     send_all(tx_g, rx_g, g1_s, g1_r)
 
@@ -196,23 +203,18 @@
 
     def inner_one(h, carry):
         cols = head_cols(h)
-        mask = causal_mask()
-        for c in range(2):
-            rows = pl.ds(c * CH, CH)
-            weights = jnp.where(mask, dot_nt(qb[rows, cols], kb[rows, cols]), 0.0).astype(BF)
-            part = dot_nn(weights, vb[rows, cols])
+        turned = vb[:, cols].T
+        for c, rows in enumerate((low, high)):
+            weights_t[h, c] = masked(dot_nt(kb[rows, cols], qb[rows, cols]), False)
+            part = dot_nn(turned[:, rows], weights_t[h, c])
             if c == 1:
-                part = part + dot_nn(qb[rows, cols], s1[h])
-            inner[rows, cols] = part
+                part = part + dot_nt(s1[h], qb[rows, cols])
+            inner_t[h, :, rows] = part
         return carry
 
     lax.fori_loop(0, count, inner_one, 0)
 
     scan(tx_g, rx_g, g1_s, g1_r, px_g, after, g2_s, g2_r, True)
-
-    finish(px_kv, before, kv2_s, kv2_r, "recv")
-    before_out = pltpu.make_async_copy(before, before_hbm, out_sem.at[1])
-    before_out.start()
 
     def mate_copy(h):
         return pltpu.make_async_remote_copy(
@@ -220,24 +222,24 @@
             recv_sem=mate_r.at[h], device_id=mate, device_id_type=MESH,
         )
 
-    def att_one(h, carry):
-        cols = head_cols(h)
-        for c in range(2):
-            rows = pl.ds(c * CH, CH)
-            total = inner[rows, cols] + dot_nn(qb[rows, cols], before[h])
-            total = total * token_factor(me, c * CH, CH)
-            att[rows, cols] = total.astype(BF)
-            turned = total.T.astype(BF)
-            for y in range(4):
-                for n in range(2):
-                    first = y * 32 + n * 16
-                    att_t[n, h, y, :, c * CH : (c + 1) * CH] = turned[first : first + 16]
+    def att_one(offset, carry):
+        h = (me + offset) % count
+
+        @pl.when(offset > 0)
+        def _():
+            arrival(px_kv, before, kv2_s, kv2_r, h).wait_recv()
+
+        total = inner_t[h] + dot_nt(before[h], qb[:, head_cols(h)])
+        total = (total * token_factor(me, (DK, 512), 1)).astype(BF)
+        att_full[h] = total
+        for y in range(4):
+            for n in range(2):
+                first = y * 32 + n * 16
+                att_t[n, h, y] = total[first : first + 16]
         mate_copy(h).start()
         return carry
 
     lax.fori_loop(0, count, att_one, 0)
-    att_out = pltpu.make_async_copy(att, att_hbm, out_sem.at[2])
-    att_out.start()
 
     og_copy.wait()
 
@@ -293,20 +295,49 @@
             rs_copy(p, 0, offset).start()
 
     finish(px_g, after, g2_s, g2_r, "recv")
-    after_out = pltpu.make_async_copy(after, after_hbm, out_sem.at[3])
-    after_out.start()
-
-    for p in range(len(PIECES)):
-        sum1[p][...] = rs_sum(p, 0).astype(BF)
-        for offset in range(1, 4):
-            rs_copy(p, 1, offset).start()
+    results = [att] + [wb.at[pl.ds(n * 512, 512)] for n in range(3)]
+    places = (att_hbm, qg_hbm, kg_hbm, vg_hbm)
+
+    def grads_one(h, carry):
+        cols = head_cols(h)
+        att[:, cols] = att_full[h].T
+        before_of = (before[h], (before[h].astype(F32) + s1[h].astype(F32)).astype(BF))
+        after_of = ((after[h].astype(F32) + g2[h].astype(F32)).astype(BF), after[h])
+        for c, rows in enumerate((low, high)):
+            qc, kc, vc, sc = qb[rows, cols], kb[rows, cols], vb[rows, cols], scaled[rows, cols]
+            mixing = masked(dot_nt(sc, vc), True)
+            mixing_t = masked(dot_nt(vc, sc), False)
+            query_grad = dot_nn(mixing, kc) + dot_nn(sc, before_of[c])
+            key_grad = dot_nn(mixing_t, qc) + dot_nt(vc, after_of[c])
+            value_grad = dot_nn(weights_t[h, c], sc) + dot_nn(kc, after_of[c])
+            wb[pl.ds(c * CH, CH), cols] = query_grad.astype(BF)
+            wb[pl.ds(512 + c * CH, CH), cols] = key_grad.astype(BF)
+            wb[pl.ds(1024 + c * CH, CH), cols] = value_grad.astype(BF)
+        return carry
+
+    def results_out(part):
+        cols = pl.ds(part * 512, 512)
+        return [
+            pltpu.make_async_copy(src.at[:, cols], dst.at[:, cols], out_sem.at[n, part])
+            for n, (src, dst) in enumerate(zip(results, places))
+        ]
+
+    for group in range(4):
+        lax.fori_loop(group * 4, group * 4 + 4, grads_one, 0)
+        for copy in results_out(group):
+            copy.start()
+        if group > 0:
+            for p in range(3 * group - 3, 3 * group):
+                sum1[p][...] = rs_sum(p, 0).astype(BF)
+                for offset in range(1, 4):
+                    rs_copy(p, 1, offset).start()
     for p in range(len(PIECES)):
         sum2[p][...] = rs_sum(p, 1).astype(BF)
         for offset in range(1, 4):
             rs_copy(p, 2, offset).start()
     for p, (first, width, order) in enumerate(PIECES):
         wgrad[:, first : first + width] = rs_sum(p, 2) * grad_scale
-    wgrad_out = pltpu.make_async_copy(wgrad, wgrad_hbm, out_sem.at[4])
+    wgrad_out = pltpu.make_async_copy(wgrad, wgrad_hbm, out_sem.at[4, 0])
     wgrad_out.start()
 
     finish(tx_kv, rx_kv, kv1_s, kv1_r, "send")
@@ -317,10 +348,9 @@
         for phase in range(3):
             for offset in range(1, 4):
                 rs_copy(p, phase, offset).wait_send()
-    scaled_out.wait()
-    before_out.wait()
-    att_out.wait()
-    after_out.wait()
+    for group in range(4):
+        for copy in results_out(group):
+            copy.wait()
     wgrad_out.wait()
 
 
@@ -333,16 +363,17 @@
     state = vm((16, DK, DK), BF)
     scratch = [
         vm((512, 2048), BF), vm((512, 2048), BF), vm((512, 2048), BF), vm((2048, 2048), BF),
-        vm((512, 2048), BF), vm((512, 2048), BF), vm((512, 2048), BF), vm((512, 2048), F32),
-        vm((512, 2048), BF), vm((2, 16, 4, 16, 512), BF), vm((16, 4, 16, 512), BF),
-        state, state, state, state, state, state, state, state, state, vm((16, 2048), F32),
+        vm((512, 2048), BF), vm((512, 2048), BF), vm((512, 2048), BF), vm((16, DK, 512), F32),
+        vm((512, 2048), BF), vm((16, DK, 512), BF), vm((2, 16, 4, 16, 512), BF),
+        vm((16, 4, 16, 512), BF), vm((16, 2, CH, CH), BF),
+        state, state, state, state, state, state, state, state, state, state, vm((16, 2048), F32),
         [vm((4, 4, 4, 16, c), BF) for c in widths],
         [vm((3, 4, 4, 16, c), BF) for c in widths],
         [vm((4, 4, 16, c), BF) for c in widths],
         [vm((3, 4, 16, c), BF) for c in widths],
         [vm((4, 16, c), BF) for c in widths],
         [vm((3, 16, c), BF) for c in widths],
-        sem((5,)), sem((5,)), sem((2,)),
+        sem((5,)), sem((5, 4)), sem((2,)),
         sem((16,)), sem((16,)), sem((16,)), sem((16,)),
         sem((16,)), sem((16,)), sem((16,)), sem((16,)),
         sem((16,)), sem((16,)), sem((3, n, 3)), sem((3, n, 3)),
@@ -352,8 +383,8 @@
         out_shape=(
             jax.ShapeDtypeStruct((512, 2048), BF),
             jax.ShapeDtypeStruct((512, 2048), BF),
-            jax.ShapeDtypeStruct((16, DK, DK), BF),
-            jax.ShapeDtypeStruct((16, DK, DK), BF),
+            jax.ShapeDtypeStruct((512, 2048), BF),
+            jax.ShapeDtypeStruct((512, 2048), BF),
             jax.ShapeDtypeStruct((16, 2048), F32),
         ),
         in_specs=[any_spec] * 5,
@@ -366,62 +397,10 @@
     )(q, k, v, w, og)
 
 
-def grads_kernel(q, k, v, s, before, after, att_hbm, qg, kg, vg, att_out, sem):
-    step = pl.program_id(0)
-    copy = pltpu.make_async_copy(att_hbm, att_out.at[0], sem)
-
-    @pl.when(step == 0)
-    def _():
-        copy.start()
-
-    mask = causal_mask()
-    low, high = slice(0, CH), slice(CH, 2 * CH)
-    for n in range(2):
-        cols = slice(n * DK, (n + 1) * DK)
-        early = dot_tn(k[0, low, cols], v[0, low, cols])
-        late = dot_tn(q[0, high, cols], s[high, cols])
-        before_of = (before[n], (before[n].astype(F32) + early).astype(BF))
-        after_of = ((after[n].astype(F32) + late).astype(BF), after[n])
-        for c, rows in enumerate((low, high)):
-            qc, kc, vc, sc = q[0, rows, cols], k[0, rows, cols], v[0, rows, cols], s[rows, cols]
-            weights = jnp.where(mask, dot_nt(qc, kc), 0.0).astype(BF)
-            mixing = jnp.where(mask, dot_nt(sc, vc), 0.0).astype(BF)
-            qg[0, rows, cols] = (dot_nn(mixing, kc) + dot_nt(sc, before_of[c])).astype(BF)
-            kg[0, rows, cols] = (dot_tn(mixing, qc) + dot_nt(vc, after_of[c])).astype(BF)
-            vg[0, rows, cols] = (dot_tn(weights, sc) + dot_nn(kc, after_of[c])).astype(BF)
-
-    @pl.when(step == pl.num_programs(0) - 1)
-    def _():
-        copy.wait()
-
-
-def grads_call(q, k, v, s, before, after, att):
-    big = pl.BlockSpec((1, 512, 256), lambda j: (0, 0, j))
-    flat = pl.BlockSpec((512, 256), lambda j: (0, j))
-    state = pl.BlockSpec((2, DK, DK), lambda j: (j, 0, 0))
-    any_spec = pl.BlockSpec(memory_space=pl.ANY)
-    shape = jax.ShapeDtypeStruct((1, 512, 2048), BF)
-    return pl.pallas_call(
-        grads_kernel,
-        grid=(8,),
-        out_shape=(shape,) * 4,
-        in_specs=[big, big, big, flat, state, state, any_spec],
-        out_specs=(big, big, big, any_spec),
-        scratch_shapes=[pltpu.SemaphoreType.DMA],
-        compiler_params=pltpu.CompilerParams(vmem_limit_bytes=32 << 20),
-        name="input_grads",
-    )(q, k, v, s, before, after, att)
-
-
 def on_device(queries, keys, values, out_weight, out_grad):
     grad_scale = 1.0 / math.sqrt(8 * 8192)
-    att, scaled, before, after, weight_grad = main_call(
-        queries, keys, values, out_weight, out_grad, grad_scale
-    )
-    query_grad, key_grad, value_grad, attended = grads_call(
-        queries, keys, values, scaled, before, after, att
-    )
-    return attended, query_grad, key_grad, value_grad, weight_grad
+    *inner, weight_grad = main_call(queries, keys, values, out_weight, out_grad, grad_scale)
+    return (*(x[None] for x in inner), weight_grad)
 
 
 def solution(mesh):

time: 101 us -> 84.1 us (0.83)
  Pallas kernels: 94.3 us -> 73.3 us
  local copies, waits for them, and re-layouts: 5.93 us -> 9.98 us
    pallas_call x1 -> x0, Pallas kernels: 14.6 us -> none  [grads_call(): pl.pallas_call(grads_kernel, grid=(8,), out_shape=(shape,) * 4, in_specs=...]
    pallas_call x1, Pallas kernels: 79.6 us -> 73.3 us  [main_call(): pl.pallas_call(functools.partial(main_kernel, grad_scale), out_shape=(jax...]
    unnamed x17 -> x13, local copies, waits for them, and re-layouts: 5.93 us -> 9.98 us
where the time goes in v2:
time: 84.1 us; the launch traced here: 84 us
  Pallas kernels  73.3 us (87%)
  local copies, waits for them, and re-layouts  9.98 us (12%)
    pallas_call x1, Pallas kernels, main_call(): pl.pallas_call(functools.partial(main_kernel, grad_scale), out_shape=(jax...  73.3 us
    unnamed x13, local copies, waits for them, and re-layouts  9.98 us

profile of v2, /device:TPU:0, one launch (start us, length us, event | category | flops | bytes accessed | tf_op | source)
XLA Modules:
  0.0 84.0 jit_solution(763789828556044730)
XLA Ops:
  0.6 73.3 %states_and_weight_grad.1 = (bf16[512,2048]{1,0:T(8,128)(2,1)}, bf16[512,2048]{1,0:T(8,128)(2,1)}, bf16[512,2048]{1,0:T(8,128)(2,1)}, bf16[512,2048]{1,0:T(8,128)(2,1)}, f32[16,2048]{1,0:T(8,128)}) custom-call(bf16[1,512,2048]{2,1,0:T(8,128)(2,1)} %q_hbm.1, bf16[1,512,2048]{2,1,0:T(8,128)(2,1)} %k_hbm.1, bf16[1,512,2048]{2,1,0:T(8,128)(2,1)} %v_hbm.1, ...), custom_call_target="tpu_custom_call" | custom-call | tf_op jit(solution)/shard_map/states_and_weight_grad/pallas_call | solution.py:381
  74.0 0.0 copy-start.2
  74.0 3.3 %copy.15 = bf16[1,512,2048]{2,1,0:T(8,128)(2,1)} copy(bf16[1,512,2048]{2,1,0:T(8,128)(2,1)} %bitcast.7) | data formatting | bytes 4194304
  77.3 0.0 copy-done.2
  77.3 0.0 copy-start.1
  77.3 1.3 %copy.16 = bf16[1,512,2048]{2,1,0:T(8,128)(2,1)} copy(bf16[1,512,2048]{2,1,0:T(8,128)(2,1)S(1)} %bitcast.6) | data formatting | bytes 4194304
  78.6 1.0 %copy-done.1 = bf16[512,2048]{1,0:T(8,128)(2,1)S(1)} copy-done((bf16[512,2048]{1,0:T(8,128)(2,1)S(1)}, bf16[512,2048]{1,0:T(8,128)(2,1)}, u32[]{:S(2)}) %copy-start.1) | copy-done | bytes 2097176
  79.6 0.0 copy-start
  79.6 1.3 %copy.17 = bf16[1,512,2048]{2,1,0:T(8,128)(2,1)} copy(bf16[1,512,2048]{2,1,0:T(8,128)(2,1)S(1)} %bitcast.5) | data formatting | bytes 4194304
  81.0 1.0 %copy-done = bf16[512,2048]{1,0:T(8,128)(2,1)S(1)} copy-done((bf16[512,2048]{1,0:T(8,128)(2,1)S(1)}, bf16[512,2048]{1,0:T(8,128)(2,1)}, u32[]{:S(2)}) %copy-start) | copy-done | bytes 2097176
  82.0 0.0 copy-start.3
  82.0 1.3 %copy.18 = bf16[1,512,2048]{2,1,0:T(8,128)(2,1)} copy(bf16[1,512,2048]{2,1,0:T(8,128)(2,1)S(1)} %bitcast.4) | data formatting | bytes 4194304
  83.3 0.0 copy-done.3
  83.3 0.7 copy.19
Async XLA Ops:
  74.0 3.3 %copy-start.2 = (bf16[512,2048]{1,0:T(8,128)(2,1)S(1)}, bf16[512,2048]{1,0:T(8,128)(2,1)}, u32[]{:S(2)}) copy-start(bf16[512,2048]{1,0:T(8,128)(2,1)} %get-tuple-element.11) | copy-start | bytes 6291460
  77.3 2.3 %copy-start.1 = (bf16[512,2048]{1,0:T(8,128)(2,1)S(1)}, bf16[512,2048]{1,0:T(8,128)(2,1)}, u32[]{:S(2)}) copy-start(bf16[512,2048]{1,0:T(8,128)(2,1)} %get-tuple-element.12) | copy-start | bytes 6291460
  79.6 2.3 %copy-start = (bf16[512,2048]{1,0:T(8,128)(2,1)S(1)}, bf16[512,2048]{1,0:T(8,128)(2,1)}, u32[]{:S(2)}) copy-start(bf16[512,2048]{1,0:T(8,128)(2,1)} %get-tuple-element.13) | copy-start | bytes 6291460
  82.0 1.3 %copy-start.3 = (f32[16,2048]{1,0:T(8,128)S(1)}, f32[16,2048]{1,0:T(8,128)}, u32[]{:S(2)}) copy-start(f32[16,2048]{1,0:T(8,128)} %get-tuple-element.24) | copy-start | bytes 393220

commit v3 on v2

v3 whole, which is shorter than its diff:
```python
import functools
import math

import jax
import jax.numpy as jnp
from jax import lax
from jax.experimental import pallas as pl
from jax.experimental.pallas import tpu as pltpu
from jax.sharding import PartitionSpec as P

DK = 128
CH = 256
MESH = pl.DeviceIdType.MESH
BF = jnp.bfloat16
F32 = jnp.float32
PIECES = (
    (0, 256, "yxz"),
    (256, 256, "xzy"),
    (512, 256, "zyx"),
    (768, 256, "yzx"),
    (1024, 256, "xyz"),
    (1280, 256, "zxy"),
    (1536, 256, "yxz"),
    (1792, 128, "xzy"),
    (1920, 128, "zyx"),
)
AXES = "xzy"


def dot_nn(a, b):
    return lax.dot_general(a, b, (((1,), (0,)), ((), ())), preferred_element_type=F32)


def dot_nt(a, b):
    return lax.dot_general(a, b, (((1,), (1,)), ((), ())), preferred_element_type=F32)


def dot_tn(a, b):
    return lax.dot_general(a, b, (((0,), (0,)), ((), ())), preferred_element_type=F32)


def head_cols(h):
    return pl.ds(pl.multiple_of(h * DK, DK), DK)


def masked(product, query_rows):
    rows = lax.broadcasted_iota(jnp.int32, (CH, CH), 0)
    cols = lax.broadcasted_iota(jnp.int32, (CH, CH), 1)
    keep = rows >= cols if query_rows else rows <= cols
    return jnp.where(keep, product, 0.0).astype(BF)


def token_factor(me, shape, axis):
    pos = me * 512 + lax.broadcasted_iota(jnp.int32, shape, axis)
    return lax.rsqrt(((pos + 1) * DK).astype(F32))


def main_kernel(
    grad_scale,
    q_hbm, k_hbm, v_hbm, w_hbm, og_hbm,
    att, qg, kg, vg, wgrad,
    qb, kb, vb, wb, og_both, scaled, inner_t, att_full, at_both, weights_t,
    s1, g2, tx_kv, rx_kv, px_kv, before, tx_g, rx_g, px_g, after,
    prod, rx1, sum1, rx2, sum2, rx3,
    in_sem, og_sem, kv1_s, kv1_r, kv2_s, kv2_r, g1_s, g1_r, g2_s, g2_r,
    mate_s, mate_r, rs_s, rs_r,
):
    me = lax.axis_index("ctx")
    dp = lax.axis_index("dp")
    place = {"x": me // 4, "z": me % 4, "y": dp // 2}
    core = dp % 2
    mate = (me, (dp // 2) * 2 + (1 - core))
    count = 16

    def axis_peer(axis, offset):
        at = dict(place)
        at[axis] = (place[axis] + offset) % 4
        return (at["x"] * 4 + at["z"], at["y"] * 2 + core)

    def by_head(first, last, one):
        def several(n, carry):
            for m in range(2):
                one(first + 2 * n + m, carry)
            return carry

        lax.fori_loop(0, (last - first) // 2, several, 0)

    loads = [
        pltpu.make_async_copy(src.at[0], dst, in_sem.at[n])
        for n, (src, dst) in enumerate(((k_hbm, kb), (v_hbm, vb), (og_hbm, og_both.at[0:512]), (q_hbm, qb)))
    ]
    loads.append(pltpu.make_async_copy(w_hbm, wb, in_sem.at[4]))
    loads[0].start()
    loads[1].start()

    barrier = pltpu.get_barrier_semaphore()
    for offset in range(1, count):
        pl.semaphore_signal(
            barrier, inc=1, device_id=((me + offset) % count, dp), device_id_type=MESH
        )
    pl.semaphore_signal(barrier, inc=1, device_id=mate, device_id_type=MESH)
    for offset in range(1, 4):
        pl.semaphore_signal(
            barrier, inc=1, device_id=axis_peer("y", offset), device_id_type=MESH
        )

    loads[0].wait()
    loads[1].wait()
    loads[2].start()
    loads[4].start()
    loads[3].start()
    low, high = slice(0, CH), slice(CH, 2 * CH)

    def pair_at(j):
        return (me // 2 + 1 + j) % (count // 2)

    def kv_one(j, carry):
        j = pair_at(j)
        wide = pl.ds(pl.multiple_of(j * 256, 256), 256)
        first = dot_tn(vb[low, wide], kb[low, wide])
        both = first + dot_tn(vb[high, wide], kb[high, wide])
        for n in range(2):
            part = slice(n * DK, (n + 1) * DK)
            s1[2 * j + n] = first[part, part].astype(BF)
            tx_kv[2 * j + n] = both[part, part].astype(BF)
        return carry

    def arrival(src, dst, send, recv, other):
        return pltpu.make_async_remote_copy(
            src_ref=src.at[other], dst_ref=dst.at[other], send_sem=send.at[other],
            recv_sem=recv.at[other], device_id=(other, dp), device_id_type=MESH,
        )

    def send_one(src, dst, send, recv, other):
        @pl.when(other != me)
        def _():
            pltpu.make_async_remote_copy(
                src_ref=src.at[other], dst_ref=dst.at[me], send_sem=send.at[other],
                recv_sem=recv.at[me], device_id=(other, dp), device_id_type=MESH,
            ).start()

    def send_all(src, dst, send, recv):
        def one(n, carry):
            send_one(src, dst, send, recv, (me + n) % count)
            return carry

        lax.fori_loop(1, count, one, 0)

    def kv_send(j, carry):
        kv_one(j, carry)
        for n in range(2):
            send_one(tx_kv, rx_kv, kv1_s, kv1_r, 2 * pair_at(j) + n)
        return carry

    def kv_sent(j, carry):
        for n in range(2):
            send_one(tx_kv, rx_kv, kv1_s, kv1_r, 2 * pair_at(j) + n)
        return carry

    lax.fori_loop(0, count // 4, kv_one, 0)
    pl.semaphore_wait(barrier, count - 1 + 1 + 3)
    lax.fori_loop(0, count // 4, kv_sent, 0)
    lax.fori_loop(count // 4, count // 2, kv_send, 0)
    rx_kv[me] = tx_kv[me]

    loads[2].wait()
    og_copy = pltpu.make_async_remote_copy(
        src_ref=og_both.at[0:512], dst_ref=og_both.at[512:1024], send_sem=og_sem.at[0], recv_sem=og_sem.at[1],
        device_id=mate, device_id_type=MESH,
    )
    og_copy.start()

    loads[4].wait()
    loads[3].wait()

    def grad_out_of(j):
        wide = pl.ds(pl.multiple_of(pair_at(j) * 256, 256), 256)
        grad_out = dot_nt(og_both[0:512], wb[wide, :]).astype(BF).astype(F32)
        scaled[:, wide] = (grad_out * token_factor(me, (512, 256), 0)).astype(BF)

    def grad_state_of(j):
        j = pair_at(j)
        wide = pl.ds(pl.multiple_of(j * 256, 256), 256)
        late = dot_tn(qb[high, wide], scaled[high, wide])
        both = late + dot_tn(qb[low, wide], scaled[low, wide])
        for n in range(2):
            part = slice(n * DK, (n + 1) * DK)
            g2[2 * j + n] = late[part, part].astype(BF)
            tx_g[2 * j + n] = both[part, part].astype(BF)
            send_one(tx_g, rx_g, g1_s, g1_r, 2 * j + n)

    def grad_one(j, carry):
        grad_state_of(j - 1)
        grad_out_of(j)
        return carry

    grad_out_of(0)
    lax.fori_loop(1, count // 2, grad_one, 0)
    grad_state_of(count // 2 - 1)
    rx_g[me] = tx_g[me]

    def scan(src, dst, send, recv, src2, dst2, send2, recv2, reverse):
        def one(n, total):
            b = count - 1 - n if reverse else n

            @pl.when(b != me)
            def _():
                arrival(src, dst, send, recv, b).wait_recv()

            src2[b] = total.astype(BF)

            return total + dst[b].astype(F32)

        lax.fori_loop(0, count, one, jnp.zeros((DK, DK), F32))
        dst2[me] = src2[me]
        send_all(src2, dst2, send2, recv2)

    def finish(src, dst, send, recv, which):
        def one(offset, carry):
            other = (me + offset) % count
            if which == "recv":
                arrival(src, dst, send, recv, other).wait_recv()
            else:
                arrival(src, dst, send, recv, other).wait_send()
            return carry

        lax.fori_loop(1, count, one, 0)

    scan(tx_kv, rx_kv, kv1_s, kv1_r, px_kv, before, kv2_s, kv2_r, False)

    def inner_one(h, carry):
        cols = head_cols(h)
        turned = vb[:, cols].T
        for c, rows in enumerate((low, high)):
            weights_t[h, c] = masked(dot_nt(kb[rows, cols], qb[rows, cols]), False)
            part = dot_nn(turned[:, rows], weights_t[h, c])
            if c == 1:
                part = part + dot_nt(s1[h], qb[rows, cols])
            inner_t[h, :, rows] = part
        return carry

    by_head(0, count, inner_one)
    scan(tx_g, rx_g, g1_s, g1_r, px_g, after, g2_s, g2_r, True)

    def mate_copy(h):
        return pltpu.make_async_remote_copy(
            src_ref=att_full.at[h, :, 1 - core], dst_ref=at_both.at[h, :, :, pl.ds(512, 512)], send_sem=mate_s.at[h],
            recv_sem=mate_r.at[h], device_id=mate, device_id_type=MESH,
        )

    def att_one(offset, carry):
        h = (me + count - offset) % count

        @pl.when(offset > 0)
        def _():
            arrival(px_kv, before, kv2_s, kv2_r, h).wait_recv()

        total = inner_t[h] + dot_nt(before[h], qb[:, head_cols(h)])
        total = (total * token_factor(me, (DK, 512), 1)).astype(BF)
        att_full[h] = total.reshape(4, 2, 16, 512)
        at_both[h, :, :, 0:512] = att_full[h, :, core]
        mate_copy(h).start()
        return carry

    lax.fori_loop(0, count, att_one, 0)

    og_copy.wait()

    def mate_wait(h, carry):
        mate_copy(h).wait()
        return carry

    lax.fori_loop(0, count, mate_wait, 0)

    def pick(ref, axes, axis, t):
        index = tuple(t if a == axis else slice(None) for a in axes)
        return ref.at[index]

    def rs_copy(p, phase, offset):
        first, width, order = PIECES[p]
        axes = [a for a in AXES if a not in order[:phase]]
        axis = order[phase]
        src = (prod, sum1, sum2)[phase][p]
        dst = (rx1, rx2, rx3)[phase][p]
        return pltpu.make_async_remote_copy(
            src_ref=pick(src, axes, axis, (place[axis] + offset) % 4),
            dst_ref=dst.at[offset - 1],
            send_sem=rs_s.at[phase, p, offset - 1],
            recv_sem=rs_r.at[phase, p, offset - 1],
            device_id=axis_peer(axis, offset), device_id_type=MESH,
        )

    def rs_sum(p, phase):
        first, width, order = PIECES[p]
        axes = [a for a in AXES if a not in order[:phase]]
        axis = order[phase]
        for offset in range(1, 4):
            rs_copy(p, phase, offset).wait_recv()
        src = (prod, sum1, sum2)[phase][p]
        dst = (rx1, rx2, rx3)[phase][p]
        total = pick(src, axes, axis, place[axis])[...].astype(F32)
        for n in range(3):
            total = total + dst[n].astype(F32)
        return total

    for p, (first, width, order) in enumerate(PIECES):
        left = at_both[...].reshape(1024, 1024)
        part = dot_nn(left, og_both[:, first : first + width])
        prod[p][...] = part.astype(BF).reshape(4, 4, 4, 16, width)
        if p < 3:
            for offset in range(1, 4):
                rs_copy(p, 0, offset).start()

    def query_one(h, carry):
        cols = head_cols(h)
        att[:, cols] = att_full[h].reshape(DK, 512).T
        before_of = (before[h], (before[h].astype(F32) + s1[h].astype(F32)).astype(BF))
        for c, rows in enumerate((low, high)):
            kc, vc, sc = kb[rows, cols], vb[rows, cols], scaled[rows, cols]
            mixing = masked(dot_nt(sc, vc), True)
            query_grad = dot_nn(mixing, kc) + dot_nn(sc, before_of[c])
            qg[rows, cols] = query_grad.astype(BF)
        return carry

    def key_one(h, carry):
        cols = head_cols(h)
        after_of = ((after[h].astype(F32) + g2[h].astype(F32)).astype(BF), after[h])
        for c, rows in enumerate((low, high)):
            qc, kc, vc, sc = qb[rows, cols], kb[rows, cols], vb[rows, cols], scaled[rows, cols]
            mixing_t = masked(dot_nt(vc, sc), False)
            key_grad = dot_nn(mixing_t, qc) + dot_nt(vc, after_of[c])
            value_grad = dot_nn(weights_t[h, c], sc) + dot_nn(kc, after_of[c])
            kg[rows, cols] = key_grad.astype(BF)
            vg[rows, cols] = value_grad.astype(BF)
        return carry

    def second_phase(pieces):
        for p in pieces:
            sum1[p][...] = rs_sum(p, 0).astype(BF)
            for offset in range(1, 4):
                rs_copy(p, 1, offset).start()

    def third_phase(pieces):
        for p in pieces:
            sum2[p][...] = rs_sum(p, 1).astype(BF)
            for offset in range(1, 4):
                rs_copy(p, 2, offset).start()

    def first_phase(pieces):
        for p in pieces:
            for offset in range(1, 4):
                rs_copy(p, 0, offset).start()

    first_phase(range(3, 6))
    by_head(0, count, query_one)
    second_phase(range(0, 3))
    first_phase(range(6, 9))
    finish(px_g, after, g2_s, g2_r, "recv")
    by_head(0, 8, key_one)
    second_phase(range(3, 6))
    by_head(8, count, key_one)
    third_phase(range(0, 3))
    second_phase(range(6, 9))
    third_phase(range(3, 9))
    for p, (first, width, order) in enumerate(PIECES):
        wgrad[:, first : first + width] = rs_sum(p, 2) * grad_scale
    finish(tx_kv, rx_kv, kv1_s, kv1_r, "send")
    finish(tx_g, rx_g, g1_s, g1_r, "send")
    finish(px_kv, before, kv2_s, kv2_r, "send")
    finish(px_g, after, g2_s, g2_r, "send")
    for p in range(len(PIECES)):
        for phase in range(3):
            for offset in range(1, 4):
                rs_copy(p, phase, offset).wait_send()

def main_call(q, k, v, w, og, grad_scale):
    any_spec = pl.BlockSpec(memory_space=pl.ANY)
    n = len(PIECES)
    widths = [width for _, width, _ in PIECES]
    vm = pltpu.VMEM
    sem = pltpu.SemaphoreType.DMA
    state = vm((16, DK, DK), BF)
    scratch = [
        vm((512, 2048), BF), vm((512, 2048), BF), vm((512, 2048), BF), vm((2048, 2048), BF),
        vm((1024, 2048), BF), vm((512, 2048), BF), vm((16, DK, 512), F32),
        vm((16, 4, 2, 16, 512), BF), vm((16, 4, 16, 1024), BF), vm((16, 2, CH, CH), BF),
        state, state, state, state, state, state, state, state, state, state,
        [vm((4, 4, 4, 16, c), BF) for c in widths],
        [vm((3, 4, 4, 16, c), BF) for c in widths],
        [vm((4, 4, 16, c), BF) for c in widths],
        [vm((3, 4, 16, c), BF) for c in widths],
        [vm((4, 16, c), BF) for c in widths],
        [vm((3, 16, c), BF) for c in widths],
        sem((5,)), sem((2,)),
        sem((16,)), sem((16,)), sem((16,)), sem((16,)),
        sem((16,)), sem((16,)), sem((16,)), sem((16,)),
        sem((16,)), sem((16,)), sem((3, n, 3)), sem((3, n, 3)),
    ]
    return pl.pallas_call(
        functools.partial(main_kernel, grad_scale),
        out_shape=(vm((512, 2048), BF),) * 4 + (vm((16, 2048), F32),),
        in_specs=[any_spec] * 5,
        out_specs=(pl.BlockSpec(memory_space=vm),) * 5,
        scratch_shapes=scratch,
        compiler_params=pltpu.CompilerParams(
            collective_id=1, has_side_effects=True, vmem_limit_bytes=50 << 20
        ),
        name="states_and_weight_grad",
    )(q, k, v, w, og)


def place_kernel(*refs):
    sem = refs[-1]
    copies = []
    for n in range(4):
        for half in range(2):
            rows = pl.ds(half * 256, 256)
            copies.append(
                pltpu.make_async_copy(
                    refs[n].at[rows], refs[5 + n].at[0, rows], sem.at[2 * n + half]
                )
            )
    copies.append(pltpu.make_async_copy(refs[4], refs[9], sem.at[8]))
    for copy in copies:
        copy.start()
    for copy in copies:
        copy.wait()


def place_call(*arrays):
    any_spec = pl.BlockSpec(memory_space=pl.ANY)
    return pl.pallas_call(
        place_kernel,
        out_shape=(jax.ShapeDtypeStruct((1, 512, 2048), BF),) * 4
        + (jax.ShapeDtypeStruct((16, 2048), F32),),
        in_specs=[pl.BlockSpec(memory_space=pltpu.VMEM)] * 5,
        out_specs=(any_spec,) * 5,
        scratch_shapes=[pltpu.SemaphoreType.DMA((9,))],
        compiler_params=pltpu.CompilerParams(vmem_limit_bytes=2 << 20),
        name="place_outputs",
    )(*arrays)


def on_device(queries, keys, values, out_weight, out_grad):
    grad_scale = 1.0 / math.sqrt(8 * 8192)
    inner = main_call(queries, keys, values, out_weight, out_grad, grad_scale)
    return place_call(*(pltpu.with_memory_space_constraint(x, pltpu.VMEM) for x in inner))


def solution(mesh):
    tokens = P("dp", "ctx", None)
    return jax.shard_map(
        on_device,
        mesh=mesh,
        in_specs=(tokens, tokens, tokens, P(), tokens),
        out_specs=(tokens, tokens, tokens, tokens, P(("ctx", "dp"), None)),
        check_vma=False,
    )
```

time: 84.1 us -> 72.4 us (0.86)
  local copies, waits for them, and re-layouts: 9.98 us -> 0 us
  Pallas kernels: 73.3 us -> 71.6 us
    unnamed x13 -> x0, local copies, waits for them, and re-layouts: 9.98 us -> none
    pallas_call x1 -> x2, Pallas kernels: 73.3 us -> 71.6 us  [the longest x1 68.3 us: main_call(): pl.pallas_call(functools.partial(main_kernel, grad_scale), out_shape=(vm(...]
where the time goes in v3:
time: 72.4 us; the launch traced here: 72.3 us
  Pallas kernels  71.6 us (99%)
    pallas_call x1, Pallas kernels, main_call(): pl.pallas_call(functools.partial(main_kernel, grad_scale), out_shape=(vm(...  68.3 us
    pallas_call x1, Pallas kernels, place_call(): pl.pallas_call(place_kernel, out_shape=(jax.ShapeDtypeStruct((1, 512, 204...  3.38 us

profile of v3, /device:TPU:0, one launch (start us, length us, event | category | flops | bytes accessed | tf_op | source)
XLA Modules:
  0.0 72.3 jit_solution(1926176211964684451)
XLA Ops:
  0.6 68.3 %states_and_weight_grad.1 = (bf16[512,2048]{1,0:T(8,128)(2,1)S(1)}, bf16[512,2048]{1,0:T(8,128)(2,1)S(1)}, bf16[512,2048]{1,0:T(8,128)(2,1)S(1)}, bf16[512,2048]{1,0:T(8,128)(2,1)S(1)}, f32[16,2048]{1,0:T(8,128)S(1)}) custom-call(bf16[1,512,2048]{2,1,0:T(8,128)(2,1)} %q_hbm.1, bf16[1,512,2048]{2,1,0:T(8,128)(2,1)} %k_hbm.1, bf16[1,512,2048]{2,1,0:T(8,128)(2,1)} %v_hbm.1, ...), custom_call_target="tpu_custom_call" | custom-call | tf_op jit(solution)/shard_map/states_and_weight_grad/pallas_call | solution.py:399
  68.9 3.4 %place_outputs.1 = (bf16[1,512,2048]{2,1,0:T(8,128)(2,1)}, bf16[1,512,2048]{2,1,0:T(8,128)(2,1)}, bf16[1,512,2048]{2,1,0:T(8,128)(2,1)}, bf16[1,512,2048]{2,1,0:T(8,128)(2,1)}, f32[16,2048]{1,0:T(8,128)}) custom-call(bf16[512,2048]{1,0:T(8,128)(2,1)S(1)} %get-tuple-element.10.refs_0_, bf16[512,2048]{1,0:T(8,128)(2,1)S(1)} %get-tuple-element.11.refs_1_, ...), custom_call_target="tpu_custom_call" | custom-call | tf_op jit(solution)/shard_map/place_outputs/pallas_call | solution.py:432

commit v4 on v3

--- a/solution.py
+++ b/solution.py
@@ -14,15 +14,12 @@
 BF = jnp.bfloat16
 F32 = jnp.float32
 PIECES = (
-    (0, 256, "yxz"),
-    (256, 256, "xzy"),
-    (512, 256, "zyx"),
-    (768, 256, "yzx"),
-    (1024, 256, "xyz"),
-    (1280, 256, "zxy"),
-    (1536, 256, "yxz"),
-    (1792, 128, "xzy"),
-    (1920, 128, "zyx"),
+    (0, 384, "yxz", 0),
+    (384, 384, "yzx", 1),
+    (768, 384, "zxy", 0),
+    (1152, 384, "zyx", 1),
+    (1536, 256, "xyz", 0),
+    (1792, 256, "xzy", 1),
 )
 AXES = "xzy"
 
@@ -61,7 +58,7 @@
     att, qg, kg, vg, wgrad,
     qb, kb, vb, wb, og_both, scaled, inner_t, att_full, at_both, weights_t,
     s1, g2, tx_kv, rx_kv, px_kv, before, tx_g, rx_g, px_g, after,
-    prod, rx1, sum1, rx2, sum2, rx3,
+    prod, rx1, sum1, rx2, sum2, rx3, middle,
     in_sem, og_sem, kv1_s, kv1_r, kv2_s, kv2_r, g1_s, g1_r, g2_s, g2_r,
     mate_s, mate_r, rs_s, rs_r,
 ):
@@ -72,9 +69,9 @@
     mate = (me, (dp // 2) * 2 + (1 - core))
     count = 16
 
-    def axis_peer(axis, offset):
+    def axis_peer(axis, to):
         at = dict(place)
-        at[axis] = (place[axis] + offset) % 4
+        at[axis] = to
         return (at["x"] * 4 + at["z"], at["y"] * 2 + core)
 
     def by_head(first, last, one):
@@ -99,9 +96,9 @@
             barrier, inc=1, device_id=((me + offset) % count, dp), device_id_type=MESH
         )
     pl.semaphore_signal(barrier, inc=1, device_id=mate, device_id_type=MESH)
-    for offset in range(1, 4):
+    for offset in (1, 3):
         pl.semaphore_signal(
-            barrier, inc=1, device_id=axis_peer("y", offset), device_id_type=MESH
+            barrier, inc=1, device_id=axis_peer("y", (place["y"] + offset) % 4), device_id_type=MESH
         )
 
     loads[0].wait()
@@ -158,7 +155,7 @@
         return carry
 
     lax.fori_loop(0, count // 4, kv_one, 0)
-    pl.semaphore_wait(barrier, count - 1 + 1 + 3)
+    pl.semaphore_wait(barrier, count - 1 + 1 + 2)
     lax.fori_loop(0, count // 4, kv_sent, 0)
     lax.fori_loop(count // 4, count // 2, kv_send, 0)
     rx_kv[me] = tx_kv[me]
@@ -169,6 +166,33 @@
         device_id=mate, device_id_type=MESH,
     )
     og_copy.start()
+
+    def scan(src, dst, send, recv, src2, dst2, send2, recv2, reverse):
+        def one(n, total):
+            b = count - 1 - n if reverse else n
+
+            @pl.when(b != me)
+            def _():
+                arrival(src, dst, send, recv, b).wait_recv()
+
+            src2[b] = total.astype(BF)
+
+            return total + dst[b].astype(F32)
+
+        lax.fori_loop(0, count, one, jnp.zeros((DK, DK), F32))
+        dst2[me] = src2[me]
+        send_all(src2, dst2, send2, recv2)
+
+    def finish(src, dst, send, recv, which):
+        def one(offset, carry):
+            other = (me + offset) % count
+            if which == "recv":
+                arrival(src, dst, send, recv, other).wait_recv()
+            else:
+                arrival(src, dst, send, recv, other).wait_send()
+            return carry
+
+        lax.fori_loop(1, count, one, 0)
 
     loads[4].wait()
     loads[3].wait()
@@ -187,7 +211,6 @@
             part = slice(n * DK, (n + 1) * DK)
             g2[2 * j + n] = late[part, part].astype(BF)
             tx_g[2 * j + n] = both[part, part].astype(BF)
-            send_one(tx_g, rx_g, g1_s, g1_r, 2 * j + n)
 
     def grad_one(j, carry):
         grad_state_of(j - 1)
@@ -195,38 +218,13 @@
         return carry
 
     grad_out_of(0)
-    lax.fori_loop(1, count // 2, grad_one, 0)
+    lax.fori_loop(1, 6, grad_one, 0)
+    scan(tx_kv, rx_kv, kv1_s, kv1_r, px_kv, before, kv2_s, kv2_r, False)
+    lax.fori_loop(6, count // 2, grad_one, 0)
     grad_state_of(count // 2 - 1)
     rx_g[me] = tx_g[me]
-
-    def scan(src, dst, send, recv, src2, dst2, send2, recv2, reverse):
-        def one(n, total):
-            b = count - 1 - n if reverse else n
-
-            @pl.when(b != me)
-            def _():
-                arrival(src, dst, send, recv, b).wait_recv()
-
-            src2[b] = total.astype(BF)
-
-            return total + dst[b].astype(F32)
-
-        lax.fori_loop(0, count, one, jnp.zeros((DK, DK), F32))
-        dst2[me] = src2[me]
-        send_all(src2, dst2, send2, recv2)
-
-    def finish(src, dst, send, recv, which):
-        def one(offset, carry):
-            other = (me + offset) % count
-            if which == "recv":
-                arrival(src, dst, send, recv, other).wait_recv()
-            else:
-                arrival(src, dst, send, recv, other).wait_send()
-            return carry
-
-        lax.fori_loop(1, count, one, 0)
-
-    scan(tx_kv, rx_kv, kv1_s, kv1_r, px_kv, before, kv2_s, kv2_r, False)
+    send_all(tx_g, rx_g, g1_s, g1_r)
+
 
     def inner_one(h, carry):
         cols = head_cols(h)
@@ -240,7 +238,6 @@
         return carry
 
     by_head(0, count, inner_one)
-    scan(tx_g, rx_g, g1_s, g1_r, px_g, after, g2_s, g2_r, True)
 
     def mate_copy(h):
         return pltpu.make_async_remote_copy(
@@ -263,6 +260,7 @@
         return carry
 
     lax.fori_loop(0, count, att_one, 0)
+    scan(tx_g, rx_g, g1_s, g1_r, px_g, after, g2_s, g2_r, True)
 
     og_copy.wait()
 
@@ -276,40 +274,61 @@
         index = tuple(t if a == axis else slice(None) for a in axes)
         return ref.at[index]
 
-    def rs_copy(p, phase, offset):
-        first, width, order = PIECES[p]
+    def partners(p, c):
+        pair = (c + 1 - 2 * (c % 2), 3 - c)
+        return pair if PIECES[p][3] == 0 else pair[::-1]
+
+    def rs_parts(p, phase):
+        order = PIECES[p][2]
         axes = [a for a in AXES if a not in order[:phase]]
         axis = order[phase]
-        src = (prod, sum1, sum2)[phase][p]
-        dst = (rx1, rx2, rx3)[phase][p]
+        return (prod, sum1, sum2)[phase][p], (rx1, rx2, rx3)[phase][p], axes, axis
+
+    def rs_copy(p, phase, slot):
+        src, dst, axes, axis = rs_parts(p, phase)
+        one, two = partners(p, place[axis])
+        if phase > 0:
+            to = (place[axis] + slot + 1) % 4
+            out = pick(src, axes, axis, to)
+        elif slot == 0:
+            out, to = pick(src, axes, axis, one), one
+        elif slot == 1:
+            out, to = pick(src, axes, axis, partners(p, one)[1]), one
+        else:
+            out, to = middle[p], two
         return pltpu.make_async_remote_copy(
-            src_ref=pick(src, axes, axis, (place[axis] + offset) % 4),
-            dst_ref=dst.at[offset - 1],
-            send_sem=rs_s.at[phase, p, offset - 1],
-            recv_sem=rs_r.at[phase, p, offset - 1],
-            device_id=axis_peer(axis, offset), device_id_type=MESH,
+            src_ref=out, dst_ref=dst.at[slot],
+            send_sem=rs_s.at[phase, p, slot], recv_sem=rs_r.at[phase, p, slot],
+            device_id=axis_peer(axis, to), device_id_type=MESH,
         )
 
+    def rs_begin(p, phase):
+        for slot in (1, 0) if phase == 0 else (0, 2, 1):
+            rs_copy(p, phase, slot).start()
+
+    def rs_mid(p):
+        src, dst, axes, axis = rs_parts(p, 0)
+        two = partners(p, place[axis])[1]
+        rs_copy(p, 0, 1).wait_recv()
+        total = pick(src, axes, axis, two)[...].astype(F32) + dst[1].astype(F32)
+        middle[p][...] = total.astype(BF)
+        rs_copy(p, 0, 2).start()
+
     def rs_sum(p, phase):
-        first, width, order = PIECES[p]
-        axes = [a for a in AXES if a not in order[:phase]]
-        axis = order[phase]
-        for offset in range(1, 4):
-            rs_copy(p, phase, offset).wait_recv()
-        src = (prod, sum1, sum2)[phase][p]
-        dst = (rx1, rx2, rx3)[phase][p]
+        src, dst, axes, axis = rs_parts(p, phase)
+        slots = (0, 2) if phase == 0 else (0, 1, 2)
+        for slot in slots:
+            rs_copy(p, phase, slot).wait_recv()
         total = pick(src, axes, axis, place[axis])[...].astype(F32)
-        for n in range(3):
-            total = total + dst[n].astype(F32)
+        for slot in slots:
+            total = total + dst[slot].astype(F32)
         return total
 
-    for p, (first, width, order) in enumerate(PIECES):
+    for p, (first, width, _, _) in enumerate(PIECES):
         left = at_both[...].reshape(1024, 1024)
         part = dot_nn(left, og_both[:, first : first + width])
         prod[p][...] = part.astype(BF).reshape(4, 4, 4, 16, width)
-        if p < 3:
-            for offset in range(1, 4):
-                rs_copy(p, 0, offset).start()
+        rs_begin(p, 0)
 
     def query_one(h, carry):
         cols = head_cols(h)
@@ -334,35 +353,20 @@
             vg[rows, cols] = value_grad.astype(BF)
         return carry
 
-    def second_phase(pieces):
-        for p in pieces:
-            sum1[p][...] = rs_sum(p, 0).astype(BF)
-            for offset in range(1, 4):
-                rs_copy(p, 1, offset).start()
-
-    def third_phase(pieces):
-        for p in pieces:
-            sum2[p][...] = rs_sum(p, 1).astype(BF)
-            for offset in range(1, 4):
-                rs_copy(p, 2, offset).start()
-
-    def first_phase(pieces):
-        for p in pieces:
-            for offset in range(1, 4):
-                rs_copy(p, 0, offset).start()
-
-    first_phase(range(3, 6))
+    def next_phase(phase):
+        for p in range(len(PIECES)):
+            (sum1, sum2)[phase - 1][p][...] = rs_sum(p, phase - 1).astype(BF)
+            rs_begin(p, phase)
+
     by_head(0, count, query_one)
-    second_phase(range(0, 3))
-    first_phase(range(6, 9))
+    for p in range(len(PIECES)):
+        rs_mid(p)
+    next_phase(1)
     finish(px_g, after, g2_s, g2_r, "recv")
-    by_head(0, 8, key_one)
-    second_phase(range(3, 6))
-    by_head(8, count, key_one)
-    third_phase(range(0, 3))
-    second_phase(range(6, 9))
-    third_phase(range(3, 9))
-    for p, (first, width, order) in enumerate(PIECES):
+    by_head(0, 10, key_one)
+    next_phase(2)
+    by_head(10, 16, key_one)
+    for p, (first, width, _, _) in enumerate(PIECES):
         wgrad[:, first : first + width] = rs_sum(p, 2) * grad_scale
     finish(tx_kv, rx_kv, kv1_s, kv1_r, "send")
     finish(tx_g, rx_g, g1_s, g1_r, "send")
@@ -370,13 +374,13 @@
     finish(px_g, after, g2_s, g2_r, "send")
     for p in range(len(PIECES)):
         for phase in range(3):
-            for offset in range(1, 4):
-                rs_copy(p, phase, offset).wait_send()
+            for slot in range(3):
+                rs_copy(p, phase, slot).wait_send()
 
 def main_call(q, k, v, w, og, grad_scale):
     any_spec = pl.BlockSpec(memory_space=pl.ANY)
     n = len(PIECES)
-    widths = [width for _, width, _ in PIECES]
+    widths = [width for _, width, _, _ in PIECES]
     vm = pltpu.VMEM
     sem = pltpu.SemaphoreType.DMA
     state = vm((16, DK, DK), BF)
@@ -391,6 +395,7 @@
         [vm((3, 4, 16, c), BF) for c in widths],
         [vm((4, 16, c), BF) for c in widths],
         [vm((3, 16, c), BF) for c in widths],
+        [vm((4, 4, 16, c), BF) for c in widths],
         sem((5,)), sem((2,)),
         sem((16,)), sem((16,)), sem((16,)), sem((16,)),
         sem((16,)), sem((16,)), sem((16,)), sem((16,)),
@@ -403,7 +408,7 @@
         out_specs=(pl.BlockSpec(memory_space=vm),) * 5,
         scratch_shapes=scratch,
         compiler_params=pltpu.CompilerParams(
-            collective_id=1, has_side_effects=True, vmem_limit_bytes=50 << 20
+            collective_id=1, has_side_effects=True, vmem_limit_bytes=52 << 20
         ),
         name="states_and_weight_grad",
     )(q, k, v, w, og)

time: 72.4 us -> 70.8 us (0.978)
  Pallas kernels: 71.6 us -> 70 us
    pallas_call x1, Pallas kernels: 68.3 us -> 66.6 us  [main_call(): pl.pallas_call(functools.partial(main_kernel, grad_scale), out_shape=(vm(...]
where the time goes in v4:
time: 70.8 us; the launch traced here: 70.6 us
  Pallas kernels  70 us (99%)
    pallas_call x1, Pallas kernels, main_call(): pl.pallas_call(functools.partial(main_kernel, grad_scale), out_shape=(vm(...  66.6 us
    pallas_call x1, Pallas kernels, place_call(): pl.pallas_call(place_kernel, out_shape=(jax.ShapeDtypeStruct((1, 512, 204...  3.38 us

profile of v4, /device:TPU:0, one launch (start us, length us, event | category | flops | bytes accessed | tf_op | source)
XLA Modules:
  0.0 70.6 jit_solution(290366109132154882)
XLA Ops:
  0.6 66.6 %states_and_weight_grad.1 = (bf16[512,2048]{1,0:T(8,128)(2,1)S(1)}, bf16[512,2048]{1,0:T(8,128)(2,1)S(1)}, bf16[512,2048]{1,0:T(8,128)(2,1)S(1)}, bf16[512,2048]{1,0:T(8,128)(2,1)S(1)}, f32[16,2048]{1,0:T(8,128)S(1)}) custom-call(bf16[1,512,2048]{2,1,0:T(8,128)(2,1)} %q_hbm.1, bf16[1,512,2048]{2,1,0:T(8,128)(2,1)} %k_hbm.1, bf16[1,512,2048]{2,1,0:T(8,128)(2,1)} %v_hbm.1, ...), custom_call_target="tpu_custom_call" | custom-call | tf_op jit(solution)/shard_map/states_and_weight_grad/pallas_call | solution.py:404
  67.2 3.4 %place_outputs.1 = (bf16[1,512,2048]{2,1,0:T(8,128)(2,1)}, bf16[1,512,2048]{2,1,0:T(8,128)(2,1)}, bf16[1,512,2048]{2,1,0:T(8,128)(2,1)}, bf16[1,512,2048]{2,1,0:T(8,128)(2,1)}, f32[16,2048]{1,0:T(8,128)}) custom-call(bf16[512,2048]{1,0:T(8,128)(2,1)S(1)} %get-tuple-element.10.refs_0_, bf16[512,2048]{1,0:T(8,128)(2,1)S(1)} %get-tuple-element.11.refs_1_, ...), custom_call_target="tpu_custom_call" | custom-call | tf_op jit(solution)/shard_map/place_outputs/pallas_call | solution.py:437

commit v5 on v4

--- a/solution.py
+++ b/solution.py
@@ -17,8 +17,8 @@
     (0, 384, "yxz", 0),
     (384, 384, "yzx", 1),
     (768, 384, "zxy", 0),
-    (1152, 384, "zyx", 1),
-    (1536, 256, "xyz", 0),
+    (1152, 256, "zyx", 1),
+    (1408, 384, "xyz", 0),
     (1792, 256, "xzy", 1),
 )
 AXES = "xzy"
@@ -245,21 +245,27 @@
             recv_sem=mate_r.at[h], device_id=mate, device_id_type=MESH,
         )
 
-    def att_one(offset, carry):
-        h = (me + count - offset) % count
-
-        @pl.when(offset > 0)
-        def _():
-            arrival(px_kv, before, kv2_s, kv2_r, h).wait_recv()
-
-        total = inner_t[h] + dot_nt(before[h], qb[:, head_cols(h)])
-        total = (total * token_factor(me, (DK, 512), 1)).astype(BF)
-        att_full[h] = total.reshape(4, 2, 16, 512)
-        at_both[h, :, :, 0:512] = att_full[h, :, core]
-        mate_copy(h).start()
-        return carry
-
-    lax.fori_loop(0, count, att_one, 0)
+    def att_some(step, carry):
+        heads = [(me + count - 2 * step - m) % count for m in range(2)]
+        for m, h in enumerate(heads):
+
+            @pl.when(2 * step + m > 0)
+            def _(h=h):
+                arrival(px_kv, before, kv2_s, kv2_r, h).wait_recv()
+
+        factor = token_factor(me, (1, 512), 1)
+        totals = [
+            ((inner_t[h] + dot_nt(before[h], qb[:, head_cols(h)])) * factor).astype(BF)
+            for h in heads
+        ]
+        for h, total in zip(heads, totals):
+            att_full[h] = total.reshape(4, 2, 16, 512)
+        for h in heads:
+            at_both[h, :, :, 0:512] = att_full[h, :, core]
+            mate_copy(h).start()
+        return carry
+
+    lax.fori_loop(0, count // 2, att_some, 0)
     scan(tx_g, rx_g, g1_s, g1_r, px_g, after, g2_s, g2_r, True)
 
     og_copy.wait()

time: 70.8 us -> 69.7 us (0.984)
  Pallas kernels: 70 us -> 68.9 us
    pallas_call x1, Pallas kernels: 66.6 us -> 65.5 us  [main_call(): pl.pallas_call(functools.partial(main_kernel, grad_scale), out_shape=(vm(...]
where the time goes in v5:
time: 69.7 us; the launch traced here: 69.6 us
  Pallas kernels  68.9 us (99%)
    pallas_call x1, Pallas kernels, main_call(): pl.pallas_call(functools.partial(main_kernel, grad_scale), out_shape=(vm(...  65.5 us
    pallas_call x1, Pallas kernels, place_call(): pl.pallas_call(place_kernel, out_shape=(jax.ShapeDtypeStruct((1, 512, 204...  3.38 us

profile of v5, /device:TPU:0, one launch (start us, length us, event | category | flops | bytes accessed | tf_op | source)
XLA Modules:
  0.0 69.6 jit_solution(16659588224272110962)
XLA Ops:
  0.6 65.5 %states_and_weight_grad.1 = (bf16[512,2048]{1,0:T(8,128)(2,1)S(1)}, bf16[512,2048]{1,0:T(8,128)(2,1)S(1)}, bf16[512,2048]{1,0:T(8,128)(2,1)S(1)}, bf16[512,2048]{1,0:T(8,128)(2,1)S(1)}, f32[16,2048]{1,0:T(8,128)S(1)}) custom-call(bf16[1,512,2048]{2,1,0:T(8,128)(2,1)} %q_hbm.1, bf16[1,512,2048]{2,1,0:T(8,128)(2,1)} %k_hbm.1, bf16[1,512,2048]{2,1,0:T(8,128)(2,1)} %v_hbm.1, ...), custom_call_target="tpu_custom_call" | custom-call | tf_op jit(solution)/shard_map/states_and_weight_grad/pallas_call | solution.py:410
  66.2 3.4 %place_outputs.1 = (bf16[1,512,2048]{2,1,0:T(8,128)(2,1)}, bf16[1,512,2048]{2,1,0:T(8,128)(2,1)}, bf16[1,512,2048]{2,1,0:T(8,128)(2,1)}, bf16[1,512,2048]{2,1,0:T(8,128)(2,1)}, f32[16,2048]{1,0:T(8,128)}) custom-call(bf16[512,2048]{1,0:T(8,128)(2,1)S(1)} %get-tuple-element.10.refs_0_, bf16[512,2048]{1,0:T(8,128)(2,1)S(1)} %get-tuple-element.11.refs_1_, ...), custom_call_target="tpu_custom_call" | custom-call | tf_op jit(solution)/shard_map/place_outputs/pallas_call | solution.py:443

commit v6 on v5

--- a/solution.py
+++ b/solution.py
@@ -309,7 +309,7 @@
         )
 
     def rs_begin(p, phase):
-        for slot in (1, 0) if phase == 0 else (0, 2, 1):
+        for slot in (0, 2, 1):
             rs_copy(p, phase, slot).start()
 
     def rs_mid(p):
@@ -334,7 +334,10 @@
         left = at_both[...].reshape(1024, 1024)
         part = dot_nn(left, og_both[:, first : first + width])
         prod[p][...] = part.astype(BF).reshape(4, 4, 4, 16, width)
-        rs_begin(p, 0)
+        rs_copy(p, 0, 1).start()
+
+    for p in range(len(PIECES)):
+        rs_copy(p, 0, 0).start()
 
     def query_one(h, carry):
         cols = head_cols(h)
@@ -364,8 +367,14 @@
             (sum1, sum2)[phase - 1][p][...] = rs_sum(p, phase - 1).astype(BF)
             rs_begin(p, phase)
 
-    by_head(0, count, query_one)
-    for p in range(len(PIECES)):
+    by_head(0, 8, query_one)
+    for p in (0, 1):
+        rs_mid(p)
+    by_head(8, 12, query_one)
+    for p in (2, 3):
+        rs_mid(p)
+    by_head(12, count, query_one)
+    for p in (4, 5):
         rs_mid(p)
     next_phase(1)
     finish(px_g, after, g2_s, g2_r, "recv")

time: 69.7 us -> 69.9 us (level)
  no operation moved by 1% of the time
where the time goes in v6:
time: 69.9 us; the launch traced here: 69.8 us
  Pallas kernels  69.1 us (99%)
    pallas_call x1, Pallas kernels, main_call(): pl.pallas_call(functools.partial(main_kernel, grad_scale), out_shape=(vm(...  65.8 us
    pallas_call x1, Pallas kernels, place_call(): pl.pallas_call(place_kernel, out_shape=(jax.ShapeDtypeStruct((1, 512, 204...  3.38 us

profile of v6, /device:TPU:0, one launch (start us, length us, event | category | flops | bytes accessed | tf_op | source)
XLA Modules:
  0.0 69.8 jit_solution(9326406070885803661)
XLA Ops:
  0.6 65.8 %states_and_weight_grad.1 = (bf16[512,2048]{1,0:T(8,128)(2,1)S(1)}, bf16[512,2048]{1,0:T(8,128)(2,1)S(1)}, bf16[512,2048]{1,0:T(8,128)(2,1)S(1)}, bf16[512,2048]{1,0:T(8,128)(2,1)S(1)}, f32[16,2048]{1,0:T(8,128)S(1)}) custom-call(bf16[1,512,2048]{2,1,0:T(8,128)(2,1)} %q_hbm.1, bf16[1,512,2048]{2,1,0:T(8,128)(2,1)} %k_hbm.1, bf16[1,512,2048]{2,1,0:T(8,128)(2,1)} %v_hbm.1, ...), custom_call_target="tpu_custom_call" | custom-call | tf_op jit(solution)/shard_map/states_and_weight_grad/pallas_call | solution.py:419
  66.4 3.4 %place_outputs.1 = (bf16[1,512,2048]{2,1,0:T(8,128)(2,1)}, bf16[1,512,2048]{2,1,0:T(8,128)(2,1)}, bf16[1,512,2048]{2,1,0:T(8,128)(2,1)}, bf16[1,512,2048]{2,1,0:T(8,128)(2,1)}, f32[16,2048]{1,0:T(8,128)}) custom-call(bf16[512,2048]{1,0:T(8,128)(2,1)S(1)} %get-tuple-element.10.refs_0_, bf16[512,2048]{1,0:T(8,128)(2,1)S(1)} %get-tuple-element.11.refs_1_, ...), custom_call_target="tpu_custom_call" | custom-call | tf_op jit(solution)/shard_map/place_outputs/pallas_call | solution.py:452
